TPU v7x, 128 devices: a whole 4x4x4 slice. The times are simulated.
128 devices in a mesh: seq: 64 (over y, z_hi, x, core), rep: 2 (over z_lo).
Axes of the slice: x: 4, y: 4, z: 4 (z_hi: 2, z_lo: 2; z = z_hi * 2 + z_lo), core: 2. Of those that a mesh axis runs over, the one named last changes fastest.
Arguments:
- layer_input: bfloat16 [2, 256, 256, 1024], P('rep', 'seq'), may hold values from -16 to 16
- out_grad: bfloat16 [2, 256, 256, 1024], P('rep', 'seq'), may hold values from -16 to 16
- slot_frame: int32 [2, 256], P('rep'), may hold values from 0 to 255, each once within a row
- ln_gain: float32 [1024], replicated, may hold values from 0.5 to 1.5
- ln_bias: float32 [1024], replicated, may hold values from -3 to 3
- w_qkv: bfloat16 [1024, 3072], replicated, may hold values from -0.1875 to 0.1875
- w_out: bfloat16 [1024, 1024], replicated, may hold values from -0.1875 to 0.1875
- time_bias: float32 [16, 511], replicated, may hold values from -4 to 240
Outputs:
- in_grad: bfloat16 [2, 256, 256, 1024], P('rep', 'seq')
- qkv_grad: float32 [1024, 3072], P(('seq', 'rep'))
- proj_grad: float32 [1024, 1024], P(('seq', 'rep'))
- gain_grad: float32 [1024], P(('seq', 'rep'))
- bias_grad: float32 [1024], P(('seq', 'rep'))
Inputs may be any that keep to these rules, and one draw needn't show every extreme that they name: For each video, slot_frame is a permutation of the frames 0 to 255.
All inputs are finite; a program needn't handle non-finite values.
Results may differ from a plain program's by a relative error of at most 0.0094.
Values may be sent and summed in bfloat16 or wider, within the bound.
No kernel may reach another device: no remote copies, remote signals or barrier semaphores. Data moves between devices by JAX's collectives and lax.ppermute only.
A program may use at most 192 MiB of HBM per device.

v0:
```python
import jax
import jax.numpy as jnp
from jax import lax
from jax.sharding import PartitionSpec as P


def expand_bias(time_bias, frames):
    offsets = (
        jnp.arange(frames, dtype=jnp.int32)[None, :]
        - jnp.arange(frames, dtype=jnp.int32)[:, None]
        + frames
        - 1
    )
    return jnp.take(time_bias, offsets, axis=1)


def position_backward(rows_in, rows_grad, ln_gain, ln_bias, w_qkv, w_out, bias_table):
    frames, positions, model_width = rows_in.shape
    head_count = bias_table.shape[0]
    head_dim = model_width // head_count
    factor = head_dim ** (-0.5)
    values_in = rows_in.astype(jnp.float32)
    row_mean = jnp.mean(values_in, axis=-1, keepdims=True)
    centred = values_in - row_mean
    inv_std = lax.rsqrt(jnp.mean(centred * centred, axis=-1, keepdims=True) + 1e-05)
    normed = centred * inv_std
    hidden = (normed * ln_gain + ln_bias).astype(jnp.bfloat16)
    flat_hidden = hidden.reshape(frames * positions, model_width)
    projected = jnp.dot(flat_hidden, w_qkv, preferred_element_type=jnp.float32).astype(jnp.bfloat16)
    projected = projected.reshape(frames, positions, 3, head_count, head_dim)
    queries = projected[:, :, 0]
    key_rows = projected[:, :, 1]
    val_rows = projected[:, :, 2]
    scores = (
        jnp.einsum("tphe,sphe->phts", queries, key_rows, preferred_element_type=jnp.float32)
        * factor
        + bias_table[None]
    )
    weights = jax.nn.softmax(scores, axis=-1)
    short_weights = weights.astype(jnp.bfloat16)
    attended = jnp.einsum(
        "phts,sphe->tphe", short_weights, val_rows, preferred_element_type=jnp.float32
    ).astype(jnp.bfloat16)
    attended = attended.reshape(frames * positions, model_width)
    flat_grad = rows_grad.reshape(frames * positions, model_width)
    att_grad = jnp.dot(flat_grad, w_out.T, preferred_element_type=jnp.float32).astype(jnp.bfloat16)
    att_grad = att_grad.reshape(frames, positions, head_count, head_dim)
    proj_term = jnp.dot(flat_grad.T, attended, preferred_element_type=jnp.float32)
    weight_grad = jnp.einsum(
        "tphe,sphe->phts", att_grad, val_rows, preferred_element_type=jnp.float32
    )
    value_grad = jnp.einsum(
        "phts,tphe->sphe", short_weights, att_grad, preferred_element_type=jnp.float32
    ).astype(jnp.bfloat16)
    score_grad = (
        weights * (weight_grad - jnp.sum(weight_grad * weights, axis=-1, keepdims=True)) * factor
    ).astype(jnp.bfloat16)
    query_grad = jnp.einsum(
        "phts,sphe->tphe", score_grad, key_rows, preferred_element_type=jnp.float32
    ).astype(jnp.bfloat16)
    key_grad = jnp.einsum(
        "phts,tphe->sphe", score_grad, queries, preferred_element_type=jnp.float32
    ).astype(jnp.bfloat16)
    packed = jnp.stack([query_grad, key_grad, value_grad], axis=2).reshape(
        frames * positions, 3 * model_width
    )
    qkv_term = jnp.dot(flat_hidden.T, packed, preferred_element_type=jnp.float32)
    hidden_grad = jnp.dot(packed, w_qkv.T, preferred_element_type=jnp.float32).reshape(
        frames, positions, model_width
    )
    gain_term = jnp.sum(hidden_grad * normed, axis=(0, 1))
    bias_term = jnp.sum(hidden_grad, axis=(0, 1))
    scaled = hidden_grad * ln_gain
    norm_grad = inv_std * (
        scaled
        - jnp.mean(scaled, axis=-1, keepdims=True)
        - normed * jnp.mean(scaled * normed, axis=-1, keepdims=True)
    )
    result = (rows_grad.astype(jnp.float32) + norm_grad).astype(jnp.bfloat16)
    return (result, qkv_term, proj_term, gain_term, bias_term)


def on_device(layer_input, out_grad, slot_frame, ln_gain, ln_bias, w_qkv, w_out, time_bias):
    local_in, local_grad = (
        lax.all_to_all(layer_input, "seq", split_axis=2, concat_axis=1, tiled=True),
        lax.all_to_all(out_grad, "seq", split_axis=2, concat_axis=1, tiled=True),
    )
    frames = local_in.shape[1]
    bias_table = expand_bias(time_bias, frames)
    frame_order = jnp.arange(frames, dtype=jnp.int32)
    inverse = jnp.zeros((frames,), jnp.int32).at[slot_frame[0]].set(frame_order)
    natural = jnp.take(local_grad[0], inverse, axis=0)
    result, qkv_term, proj_term, gain_term, bias_term = position_backward(
        local_in[0], natural, ln_gain, ln_bias, w_qkv, w_out, bias_table
    )
    in_grad = lax.all_to_all(result[None], "seq", split_axis=1, concat_axis=2, tiled=True)
    tokens = (
        layer_input.shape[0]
        * layer_input.shape[1]
        * layer_input.shape[2]
        * lax.axis_size("seq")
        * lax.axis_size("rep")
    )
    factor = float(tokens) ** (-0.5)
    grad_terms = (qkv_term * factor, proj_term * factor, gain_term * factor, bias_term * factor)
    grad_sums = (
        lax.psum_scatter(grad_terms[0], ("seq", "rep"), scatter_dimension=0, tiled=True),
        lax.psum_scatter(grad_terms[1], ("seq", "rep"), scatter_dimension=0, tiled=True),
        lax.psum_scatter(grad_terms[2], ("seq", "rep"), scatter_dimension=0, tiled=True),
        lax.psum_scatter(grad_terms[3], ("seq", "rep"), scatter_dimension=0, tiled=True),
    )
    return (in_grad, grad_sums[0], grad_sums[1], grad_sums[2], grad_sums[3])


def solution(mesh):
    return jax.shard_map(
        on_device,
        mesh=mesh,
        in_specs=(
            P("rep", "seq", None, None),
            P("rep", "seq", None, None),
            P("rep", None),
            P(),
            P(),
            P(),
            P(),
            P(),
        ),
        out_specs=(
            P("rep", "seq", None, None),
            P(("seq", "rep"), None),
            P(("seq", "rep"), None),
            P(("seq", "rep")),
            P(("seq", "rep")),
        ),
        check_vma=False,
    )
```

profile of v0, /device:TPU:0, one launch (start us, length us, event | category | flops | bytes accessed | tf_op | source)
XLA Modules:
  0.0 1849.9 jit_solution(18026604118959795066)
XLA Ops:
  7.2 4.7 copy.54
  11.9 11.6 all-to-all-start.1
  23.8 217.0 %gather_fusion.1 = f32[65536,16]{1,0:T(8,128)} fusion(f32[16,511]{0,1:T(8,128)S(1)} %copy.59, s32[65536]{0:T(1024)S(1)} %broadcast_clamp_fusion), kind=kCustom, calls=%fused_computation.1 | custom fusion | bytes 8650752 | tf_op jit(solution)/shard_map/jit(_take)/gather | solution.py:14
  240.8 20.0 %copy.60 = f32[256,256,16]{0,1,2:T(8,128)} copy(f32[256,256,16]{2,1,0:T(8,128)} %bitcast.85) | data formatting | bytes 8388608 | tf_op jit(solution)/shard_map/jit(_take)/gather | solution.py:14
  260.9 4.6 copy.51
  267.7 4.6 select_bitcast_fusion
  272.3 10.5 all-to-all-start
  283.4 2.8 convert.8
  286.2 2.9 bitcast_reduce_fusion
  291.9 4.6 copy.106
  296.8 5.3 reshape.232
  302.1 12.3 convolution_convert_fusion
  314.4 16.0 reshape.228
  330.3 9.1 fusion.67
  339.4 5.9 copy.85
  345.3 5.9 copy.86
  351.2 6.0 copy.87
  357.2 4.0 copy.52
  361.2 5.2 gather_fusion
  366.4 3.9 gather.12
  370.4 5.3 fusion.37
  375.7 6.3 reshape.229
  382.1 6.0 copy.62
  388.1 4.1 fusion.25
  392.2 8.1 fusion.68
  400.4 8.1 fusion.22
  408.5 23.8 %convert_bitcast_fusion.3 = bf16[256,4,1,16,64]{0,4,3,1,2:T(8,128)(2,1)} fusion(f32[4,16,256,256]{2,3,1,0:T(8,128)} %fusion.22, bf16[256,4,1,16,64]{0,4,3,1,2:T(8,128)(2,1)} %copy.85, f32[4,16,256,256]{2,3,1,0:T(8,128)} %get-tuple-element.17, f32[4,16,256]{2,1,0:T(8,128)S(1)} %get-tuple-element.16), kind=kOutput, calls=%fused_computation.48 | convolution fusion | flops 567296256 | bytes 37814272 | tf_op jit(solution)/shard_map/phts,sphe->tphe/dot_general | solution.py:58
  432.4 23.9 %convert_bitcast_fusion.2 = bf16[256,4,1,16,64]{0,4,3,1,2:T(8,128)(2,1)} fusion(f32[4,16,256,256]{2,3,1,0:T(8,128)} %fusion.22, bf16[256,4,1,16,64]{0,4,3,1,2:T(8,128)(2,1)} %copy.86, f32[4,16,256,256]{2,3,1,0:T(8,128)} %get-tuple-element.17, f32[4,16,256]{2,1,0:T(8,128)S(1)} %get-tuple-element.16), kind=kOutput, calls=%fused_computation.47 | convolution fusion | flops 567296256 | bytes 37814272 | tf_op jit(solution)/shard_map/phts,tphe->sphe/dot_general | solution.py:61
  456.3 9.1 convert_bitcast_fusion.1
  465.3 4.7 copy.55
  470.0 8.8 convert_bitcast_fusion
  479.6 3.3 copy.67
  484.6 7.1 copy.76
  491.7 6.5 reshape.231
  498.2 14.8 multiply_reduce_fusion.1
  513.0 4.5 fusion.35
  521.4 6.6 convolution_multiply_fusion.1
  528.1 18.5 %copy.73 = bf16[256,4,3,16,64]{4,3,2,1,0:T(8,128)(2,1)} copy(bf16[256,4,3,16,64]{0,4,3,1,2:T(8,128)(2,1)} %copy-done.4) | data formatting | bytes 12582912 | tf_op jit(solution)/shard_map/stack | solution.py:64
  546.6 16.3 reshape.230
  563.0 6.1 add_convert_fusion
  571.2 12.2 convolution_multiply_fusion
  585.0 2.9 copy.71
  587.9 10.6 all-to-all-start.2
  598.5 83.7 %all-reduce.2 = (f32[1024]{0:T(1024)S(1)}, f32[1024]{0:T(1024)S(1)}) all-reduce(f32[1024]{0:T(1024)S(1)} %get-tuple-element.20, f32[1024]{0:T(1024)S(1)} %get-tuple-element.19), channel_id=4, replica_groups=mesh['seq'=64,'rep'=2] {'seq','rep'}, use_global_device_ids=true, to_apply=%region_11.12.clone | all-reduce | flops 2048 | bytes 16384
  683.5 3.9 copy.72
  687.3 4.0 all_to_all.38
  691.3 493.7 %reduce-scatter.5.cloned.1.call-done = f32[8,1024]{1,0:T(8,128)} async-done(((f32[1024,1024]{1,0:T(8,128)}), f32[8,1024]{1,0:T(8,128)}) %reduce-scatter.5.cloned.1.call-update) | async-done | bytes 32784 | tf_op jit(solution)/shard_map/reduce_scatter | solution.py:108
  1185.0 657.8 %reduce-scatter.3.cloned.1.call-done = f32[8,3072]{1,0:T(8,128)} async-done(((f32[1024,3072]{1,0:T(8,128)}), f32[8,3072]{1,0:T(8,128)}) %reduce-scatter.3.cloned.1.call-update) | async-done | bytes 98320 | tf_op jit(solution)/shard_map/reduce_scatter | solution.py:107
  (87 shorter events, 17.3 us)
Async XLA Ops:
  7.2 363.2 %copy-start = (bf16[1024,1024]{1,0:T(8,128)(2,1)S(1)}, bf16[1024,1024]{1,0:T(8,128)(2,1)}, u32[]{:S(2)}) copy-start(bf16[1024,1024]{1,0:T(8,128)(2,1)} %param.14) | copy-start | bytes 6291460
  7.2 16.5 copy-start.18
  11.9 260.4 %all-to-all-start.1 = ((bf16[1,4,256,1024]{3,1,0,2:T(4,128)(2,1)}), bf16[1,4,256,1024]{3,1,0,2:T(4,128)(2,1)}, u32[]{:S(2)}, u32[]{:S(2)}) async-start(bf16[1,4,256,1024]{3,1,0,2:T(4,128)(2,1)} %copy.54), calls=%async_computation.1 | async-start | bytes 4194304 | tf_op jit(solution)/shard_map/all_to_all | solution.py:85
  260.9 4.6 copy-start.25
  266.9 0.5 copy-start.23
  272.3 84.9 %all-to-all-start = ((bf16[1,4,256,1024]{3,1,0,2:T(4,128)(2,1)}), bf16[1,4,256,1024]{3,1,0,2:T(4,128)(2,1)}, u32[]{:S(2)}, u32[]{:S(2)}) async-start(bf16[1,4,256,1024]{3,1,0,2:T(4,128)(2,1)} %copy.51), calls=%async_computation | async-start | bytes 4194304 | tf_op jit(solution)/shard_map/all_to_all | solution.py:86
  282.9 902.1 %reduce-scatter.5.cloned.1.call-start = ((), (), s32[]{:S(2)}) async-start(), calls=%async_computation.6 | async-start | bytes 4227072 | tf_op jit(solution)/shard_map/reduce_scatter | solution.py:108
  286.2 2.9 copy-start.3
  289.1 7.4 copy-start.11
  296.6 5.5 copy-start.14
  296.8 5.3 copy-start.19
  296.8 5.3 copy-start.21
  382.1 6.0 copy-start.8
  388.1 4.1 copy-start.2
  392.2 8.2 copy-start.7
  392.2 8.2 copy-start.9
  470.0 8.8 copy-start.16
  470.0 8.8 copy-start.17
  479.5 4.9 copy-start.4
  479.5 4.9 copy-start.15
  479.5 5.0 copy-start.12
  479.6 5.0 copy-start.13
  491.7 6.5 copy-start.20
  498.2 14.8 copy-start.5
  498.2 14.8 copy-start.6
  498.2 14.8 copy-start.24
  528.1 1314.8 %reduce-scatter.3.cloned.1.call-start = ((), (), s32[]{:S(2)}) async-start(), calls=%async_computation.5 | async-start | bytes 12681216 | tf_op jit(solution)/shard_map/reduce_scatter | solution.py:107
  546.6 16.3 copy-start.22
  583.4 1.6 copy-start.10
  587.9 95.5 %all-to-all-start.2 = ((bf16[1,256,4,1024]{3,2,0,1:T(4,128)(2,1)}), bf16[1,256,4,1024]{3,2,0,1:T(4,128)(2,1)}, u32[]{:S(2)}, u32[]{:S(2)}) async-start(bf16[1,256,4,1024]{3,2,0,1:T(4,128)(2,1)} %copy.71), calls=%async_computation.2 | async-start | bytes 4194304 | tf_op jit(solution)/shard_map/all_to_all | solution.py:96
  683.5 1159.4 %copy-start.1 = (bf16[1024,1024]{1,0:T(8,128)(2,1)S(1)}, bf16[1024,1024]{1,0:T(8,128)(2,1)}, u32[]{:S(2)}) copy-start(bf16[1024,1024]{1,0:T(8,128)(2,1)} %param.14) | copy-start | bytes 6291460
Sparse Core Ops, SparseCore 0:
  528.2 656.7 reduce-scatter.4
  1188.1 654.7 reduce-scatter.2
where the time goes:
time: 1860 us; the launch traced here: 1850 us
  waiting for transfers between devices  1150 us (62%)
  local copies, waits for them, and re-layouts  405 us (22%)
  matrix products  129 us (7%)
  blocking collectives  83.7 us (4%)
  starting transfers between devices  33.3 us (2%)
  other arithmetic  32.7 us (2%)
    reduce_scatter x1, waiting for transfers between devices, on_device(): lax.psum_scatter(grad_terms[0], ('seq', 'rep'), scatter_dimension=0, tile...  658 us
    reduce_scatter x1, waiting for transfers between devices, on_device(): lax.psum_scatter(grad_terms[1], ('seq', 'rep'), scatter_dimension=0, tile...  494 us
    gather x2, local copies, waits for them, and re-layouts, expand_bias(): return jnp.take(time_bias, offsets, axis=1)  237 us
    unnamed x1, blocking collectives  83.7 us
  transfers between devices with their start and end apart: 5, of which 2 were waited for; matrix products, arithmetic and copies ran while one was open for 21% of the time, Pallas kernels for 0%

commit v1 on v0

v1 whole, which is shorter than its diff:
```python
import functools

import jax
import jax.numpy as jnp
from jax import lax
from jax.experimental import pallas as pl
from jax.experimental.pallas import tpu as pltpu
from jax.sharding import Mesh, PartitionSpec as P

BF = jnp.bfloat16
F32 = jnp.float32
VMEM_BYTES = 60 * 1024 * 1024
SPAN = 4
GROUP = 16
PAIR = 128
SEQ = ("y", "zh", "x", "core")
CHIPS = ("y", "zh", "x", "zl")

NT = (((1,), (1,)), ((), ()))
TN = (((0,), (0,)), ((), ()))


def mm(a, b, dims=(((1,), (0,)), ((), ()))):
    return lax.dot_general(a, b, dims, preferred_element_type=F32)


def params(*semantics):
    return pltpu.CompilerParams(vmem_limit_bytes=VMEM_BYTES)


def cost(flops, moved, transcendentals=0):
    return pl.CostEstimate(flops=flops, bytes_accessed=moved, transcendentals=transcendentals)


def full(shape):
    return pl.BlockSpec(shape, lambda *ids: (0,) * len(shape))


def digits(index, *sizes):
    out = []
    for size in reversed(sizes):
        out.append(lax.rem(index, size))
        index = lax.div(index, size)
    return out[::-1]


def one_hot_rows(targets, shape, axis):
    return (targets == lax.broadcasted_iota(jnp.int32, shape, axis)).astype(F32).astype(BF)


def frame_major_from(shape):
    row = lax.broadcasted_iota(jnp.int32, shape, 0)
    block, place, frame = digits(row, GROUP, SPAN, SPAN)
    return one_hot_rows((frame * GROUP + block) * SPAN + place, shape, 1)


def frame_major_to(shape):
    col = lax.broadcasted_iota(jnp.int32, shape, 1)
    block, place, frame = digits(col, GROUP, SPAN, SPAN)
    return one_hot_rows((frame * GROUP + block) * SPAN + place, shape, 0)


def place_major_from(shape):
    col = lax.broadcasted_iota(jnp.int32, shape, 1)
    block, place, frame = digits(col, GROUP, SPAN, SPAN)
    return one_hot_rows((place * GROUP + block) * SPAN + frame, shape, 0)


def place_major_to(shape):
    row = lax.broadcasted_iota(jnp.int32, shape, 0)
    block, place, frame = digits(row, GROUP, SPAN, SPAN)
    return one_hot_rows((place * GROUP + block) * SPAN + frame, shape, 1)


SQUARE = (GROUP * SPAN * SPAN, GROUP * SPAN * SPAN)


def split_kernel(rows_ref, out_ref):
    spread = rows_ref[0].reshape(SQUARE[0], rows_ref.shape[-1])
    moved = mm(frame_major_from(SQUARE), spread).astype(BF)
    out_ref[...] = moved.reshape(out_ref.shape)


def split_patches(rows):
    _, span, patches, width = rows.shape
    blocks = patches // span
    return pl.pallas_call(
        split_kernel,
        grid=(blocks // GROUP,),
        in_specs=[pl.BlockSpec((1, span, GROUP * span, width), lambda c: (0, 0, c, 0))],
        out_specs=pl.BlockSpec((GROUP, span * span, width), lambda c: (c, 0, 0)),
        out_shape=jax.ShapeDtypeStruct((blocks, span * span, width), BF),
        compiler_params=params(),
        cost_estimate=cost(2 * 256 * rows.size, 4 * rows.size),
        name="split_patches",
    )(rows)


def merge_kernel(rows_ref, out_ref):
    moved = mm(frame_major_to(SQUARE), rows_ref[...].reshape(SQUARE[0], rows_ref.shape[-1]))
    out_ref[0] = moved.astype(BF).reshape(out_ref.shape[1:])


def merge_patches(rows):
    blocks, rows_each, width = rows.shape
    return pl.pallas_call(
        merge_kernel,
        grid=(blocks // GROUP,),
        in_specs=[pl.BlockSpec((GROUP, rows_each, width), lambda c: (c, 0, 0))],
        out_specs=pl.BlockSpec((1, SPAN, GROUP * SPAN, width), lambda c: (0, 0, c, 0)),
        out_shape=jax.ShapeDtypeStruct((1, SPAN, blocks * SPAN, width), BF),
        compiler_params=params(),
        cost_estimate=cost(2 * 256 * rows.size, 4 * rows.size),
        name="merge_patches",
    )(rows)


def bias_kernel(bias_ref, out_ref):
    frames = out_ref.shape[-1]
    wide = jnp.broadcast_to(bias_ref[0], (frames, 2 * frames))
    rolled = pltpu.roll(wide, frames + 1, 1, stride=1, stride_axis=0)
    out_ref[0] = rolled[:, :frames]


def expand_bias(time_bias, frames):
    heads = time_bias.shape[0]
    turned = jnp.pad(time_bias[:, ::-1], ((0, 0), (0, 1))).reshape(heads, 1, 2 * frames)
    return pl.pallas_call(
        bias_kernel,
        grid=(heads,),
        in_specs=[pl.BlockSpec((1, 1, 2 * frames), lambda h: (h, 0, 0))],
        out_specs=pl.BlockSpec((1, frames, frames), lambda h: (h, 0, 0)),
        out_shape=jax.ShapeDtypeStruct((heads, frames, frames), F32),
        compiler_params=params(),
        cost_estimate=cost(heads * frames * frames * 8, 4 * heads * frames * frames),
        name="expand_bias",
    )(turned)


def gather_places(rows_ref, out_ref):
    blocks, _, width = rows_ref.shape
    order = place_major_from(SQUARE)
    run = GROUP * SPAN
    for c in range(blocks // GROUP):
        chunk = rows_ref[c * GROUP : (c + 1) * GROUP].reshape(SQUARE[0], width)
        moved = mm(order, chunk).astype(BF)
        for p in range(SPAN):
            out_ref[p, c * run : (c + 1) * run, :] = moved[p * run : (p + 1) * run, :]


def norm_parts(values):
    mean = jnp.mean(values, axis=-1, keepdims=True)
    centred = values - mean
    inv_std = lax.rsqrt(jnp.mean(centred * centred, axis=-1, keepdims=True) + 1e-05)
    return centred * inv_std, inv_std


def halves(frames):
    return lax.broadcasted_iota(jnp.int32, (frames, PAIR), 1) < PAIR // 2


def forward_kernel(
    rows_ref, gain_ref, bias_ref, w_ref, table_ref, order_ref,
    places_ref, turned_ref, proj_ref, weights_ref, att_ref, places,
):
    step = pl.program_id(0)

    @pl.when(step == 0)
    def _():
        gather_places(rows_ref, places)

    rows = places[step]
    places_ref[0] = rows
    normed, _ = norm_parts(rows.astype(F32))
    hidden = (normed * gain_ref[...] + bias_ref[...]).astype(BF)
    turned_ref[...] = mm(order_ref[...], hidden, NT).astype(BF)
    width = hidden.shape[1]
    factor = 0.125
    proj_ref[0, :, :width] = (mm(hidden, w_ref[:, :width]) * factor).astype(BF)
    proj_ref[0, :, width : 2 * width] = mm(hidden, w_ref[:, width : 2 * width]).astype(BF)
    proj_ref[0, :, 2 * width :] = mm(hidden, w_ref[:, 2 * width :]).astype(BF)
    frames = rows.shape[0]
    first = halves(frames)
    upper = lax.broadcasted_iota(jnp.int32, (PAIR, frames), 0) < PAIR // 2
    for i in range(width // PAIR):
        lanes = slice(i * PAIR, (i + 1) * PAIR)
        queries = proj_ref[0, :, lanes]
        keys = proj_ref[0, :, width + i * PAIR : width + (i + 1) * PAIR]
        vals = proj_ref[0, :, 2 * width + i * PAIR : 2 * width + (i + 1) * PAIR]
        parts = []
        for h in range(2):
            mine = jnp.where(first if h == 0 else ~first, keys, jnp.zeros_like(keys))
            scores = mm(mine, queries, NT) + table_ref[2 * i + h]
            top = jnp.max(scores, axis=0, keepdims=True)
            raised = jnp.exp(scores - top)
            total = jnp.sum(raised, axis=0, keepdims=True)
            short = (raised * (1.0 / total)).astype(BF)
            weights_ref[0, 2 * i + h] = short
            parts.append(mm(vals, short, TN))
        att_ref[0, :, lanes] = jnp.where(upper, parts[0], parts[1]).T.astype(BF)


def forward(rows, gain, bias, w_qkv, table, order):
    blocks, _, width = rows.shape
    frames = blocks * SPAN
    heads = table.shape[0]
    per = lambda *tail: pl.BlockSpec((1,) + tail, lambda p: (p,) + (0,) * len(tail))
    return pl.pallas_call(
        forward_kernel,
        grid=(SPAN,),
        in_specs=[full(rows.shape), full((1, width)), full((1, width)), full(w_qkv.shape),
                  full(table.shape), full(order.shape)],
        out_specs=[
            per(frames, width),
            pl.BlockSpec((width, frames), lambda p: (0, p)),
            per(frames, 3 * width),
            per(heads, frames, frames),
            per(frames, width),
        ],
        out_shape=[
            jax.ShapeDtypeStruct((SPAN, frames, width), BF),
            jax.ShapeDtypeStruct((width, SPAN * frames), BF),
            jax.ShapeDtypeStruct((SPAN, frames, 3 * width), BF),
            jax.ShapeDtypeStruct((SPAN, heads, frames, frames), BF),
            jax.ShapeDtypeStruct((SPAN, frames, width), BF),
        ],
        scratch_shapes=[pltpu.VMEM((SPAN, frames, width), BF)],
        compiler_params=params(),
        cost_estimate=cost(16 * 10**9, 34 * 2**20, 2**22),
        name="forward",
    )(rows, gain, bias, w_qkv, table, order)


def values_kernel(
    rows_ref, slot_ref, w_ref, weights_ref, att_ref, turned_ref, order_ref,
    grad_ref, att_grad_ref, val_grad_ref, keep_ref, send_ref, places, turned_grad, val_grads,
):
    step = pl.program_id(0)

    @pl.when(step == 0)
    def _():
        gather_places(rows_ref, places)

    frames, width = places.shape[1:]
    natural = one_hot_rows(slot_ref[...], (frames, frames), 0)
    grads = mm(natural, places[step]).astype(BF)
    grad_ref[0] = grads
    here = pl.ds(pl.multiple_of(step * frames, frames), frames)
    turned_grad[:, here] = mm(order_ref[...], grads, NT).astype(BF)
    att_grad_ref[0] = mm(grads, w_ref[...], NT).astype(BF)
    first = halves(frames)
    for i in range(width // PAIR):
        lanes = slice(i * PAIR, (i + 1) * PAIR)
        att_grad = att_grad_ref[0, :, lanes]
        parts = [mm(weights_ref[0, 2 * i + h], att_grad) for h in range(2)]
        merged = jnp.where(first, parts[0], parts[1]).astype(BF)
        val_grad_ref[0, :, lanes] = merged
        val_grads[here, lanes] = merged

    @pl.when(step == pl.num_programs(0) - 1)
    def _():
        half = width // 2
        chunk = 256
        for c in range(width // chunk):
            cols = slice(c * chunk, (c + 1) * chunk)
            after = slice(width + c * chunk, width + (c + 1) * chunk)
            term = mm(turned_ref[...], val_grads[:, cols]).astype(BF)
            keep_ref[:, cols] = term[:half]
            send_ref[:, cols] = term[half:]
            att = att_ref[:, :, cols].reshape(SPAN * frames, chunk)
            term = mm(turned_grad[...], att).astype(BF)
            keep_ref[:, after] = term[:half]
            send_ref[:, after] = term[half:]


def values_backward(rows, slot_frame, w_out, weights, att, turned, order):
    blocks, _, width = rows.shape
    frames = blocks * SPAN
    heads = weights.shape[1]
    tokens = SPAN * frames
    per = lambda *tail: pl.BlockSpec((1,) + tail, lambda p: (p,) + (0,) * len(tail))
    rows_each = jax.ShapeDtypeStruct((SPAN, frames, width), BF)
    half = jax.ShapeDtypeStruct((width // 2, 2 * width), BF)
    return pl.pallas_call(
        values_kernel,
        grid=(SPAN,),
        in_specs=[full(rows.shape), full(slot_frame.shape), full(w_out.shape), per(heads, frames, frames),
                  full(att.shape), full(turned.shape), full(order.shape)],
        out_specs=[per(frames, width), per(frames, width), per(frames, width), full(half.shape), full(half.shape)],
        out_shape=[rows_each, rows_each, rows_each, half, half],
        scratch_shapes=[
            pltpu.VMEM((SPAN, frames, width), BF),
            pltpu.VMEM((width, tokens), BF),
            pltpu.VMEM((tokens, width), BF),
        ],
        compiler_params=params(),
        cost_estimate=cost(12 * 10**9, 28 * 2**20),
        name="values_backward",
    )(rows, slot_frame, w_out, weights, att, turned, order)


def scores_kernel(
    weights_ref, proj_ref, att_grad_ref, val_grad_ref, grad_ref, places_ref, w_ref, gain_ref,
    pair_ref, out_ref, sums_ref, results,
):
    step = pl.program_id(0)
    frames, width = grad_ref.shape[1:]
    first = halves(frames)
    upper = lax.broadcasted_iota(jnp.int32, (PAIR, frames), 0) < PAIR // 2
    factor = 0.125
    for i in range(width // PAIR):
        lanes = slice(i * PAIR, (i + 1) * PAIR)
        key_lanes = slice(width + i * PAIR, width + (i + 1) * PAIR)
        queries = proj_ref[0, :, lanes]
        keys = proj_ref[0, :, key_lanes]
        vals = proj_ref[0, :, 2 * width + i * PAIR : 2 * width + (i + 1) * PAIR]
        att_grad = att_grad_ref[0, :, lanes]
        key_parts, query_parts = [], []
        for h in range(2):
            mine = jnp.where(first if h == 0 else ~first, vals, jnp.zeros_like(vals))
            weight_grad = mm(mine, att_grad, NT)
            weights = weights_ref[0, 2 * i + h].astype(F32)
            shared = jnp.sum(weight_grad * weights, axis=0, keepdims=True)
            score_grad = (weights * (weight_grad - shared)).astype(BF)
            key_parts.append(mm(score_grad, queries))
            query_parts.append(mm(keys, score_grad, TN))
        pair_ref[0, :, lanes] = (jnp.where(upper, query_parts[0], query_parts[1]) * factor).T.astype(BF)
        pair_ref[0, :, key_lanes] = jnp.where(first, key_parts[0], key_parts[1]).astype(BF)

    hidden_grad = mm(pair_ref[0], w_ref[:, : 2 * width], NT) + mm(val_grad_ref[0], w_ref[:, 2 * width :], NT)
    normed, inv_std = norm_parts(places_ref[0].astype(F32))
    scaled = hidden_grad * gain_ref[...]
    norm_grad = inv_std * (
        scaled
        - jnp.mean(scaled, axis=-1, keepdims=True)
        - normed * jnp.mean(scaled * normed, axis=-1, keepdims=True)
    )
    results[step] = (grad_ref[0].astype(F32) + norm_grad).astype(BF)
    gain_term = jnp.sum(hidden_grad * normed, axis=0, keepdims=True)
    bias_term = jnp.sum(hidden_grad, axis=0, keepdims=True)

    @pl.when(step == 0)
    def _():
        sums_ref[...] = jnp.zeros_like(sums_ref)

    sums_ref[0:1, :] += gain_term
    sums_ref[1:2, :] += bias_term

    @pl.when(step == pl.num_programs(0) - 1)
    def _():
        order = place_major_to(SQUARE)
        run = GROUP * SPAN
        for c in range(frames // run):
            chunk = results[:, c * run : (c + 1) * run, :].reshape(SQUARE[0], width)
            moved = mm(order, chunk).astype(BF)
            out_ref[c * GROUP : (c + 1) * GROUP] = moved.reshape(GROUP, SPAN * SPAN, width)


def scores_backward(weights, proj, att_grad, val_grad, grads, places, w_qkv, gain):
    _, frames, width = grads.shape
    heads = weights.shape[1]
    blocks = frames // SPAN
    per = lambda *tail: pl.BlockSpec((1,) + tail, lambda p: (p,) + (0,) * len(tail))
    return pl.pallas_call(
        scores_kernel,
        grid=(SPAN,),
        in_specs=[per(heads, frames, frames), per(frames, 3 * width), per(frames, width), per(frames, width),
                  per(frames, width), per(frames, width), full(w_qkv.shape), full((1, width))],
        out_specs=[per(frames, 2 * width), full((blocks, SPAN * SPAN, width)), full((8, width))],
        out_shape=[
            jax.ShapeDtypeStruct((SPAN, frames, 2 * width), BF),
            jax.ShapeDtypeStruct((blocks, SPAN * SPAN, width), BF),
            jax.ShapeDtypeStruct((8, width), F32),
        ],
        scratch_shapes=[pltpu.VMEM((SPAN, frames, width), BF)],
        compiler_params=params(),
        cost_estimate=cost(18 * 10**9, 34 * 2**20),
        name="scores_backward",
    )(weights, proj, att_grad, val_grad, grads, places, w_qkv, gain)


def pair_kernel(turned_ref, pair_ref, order_ref, sums_ref, keep_ref, send_ref):
    width, tokens = turned_ref.shape
    half = width // 2
    chunk = 256
    columns = pair_ref.shape[-1]
    for c in range(columns // chunk):
        cols = slice(c * chunk, (c + 1) * chunk)
        block = pair_ref[:, :, cols].reshape(tokens, chunk)
        term = mm(turned_ref[...], block).astype(BF)
        keep_ref[:, cols] = term[:half]
        send_ref[:, cols] = term[half:]
    sums = sums_ref[...]
    high = sums.astype(BF)
    low = (sums - high.astype(F32)).astype(BF)
    both = jnp.concatenate([high.astype(F32), low.astype(F32)], axis=0)
    spread = jnp.concatenate([both, jnp.zeros((PAIR - 16, width), F32)], axis=0).astype(BF)
    term = mm(order_ref[...], spread, NT).astype(BF)
    keep_ref[:, columns:] = term[:half]
    send_ref[:, columns:] = term[half:]


def pair_terms(turned, pair, order, sums):
    width, tokens = turned.shape
    columns = pair.shape[-1]
    half = jax.ShapeDtypeStruct((width // 2, columns + PAIR), BF)
    return pl.pallas_call(
        pair_kernel,
        out_shape=[half, half],
        compiler_params=params(),
        cost_estimate=cost(2 * width * tokens * columns, 14 * 2**20),
        name="pair_terms",
    )(turned, pair, order, sums)


def row_order(width):
    row = jnp.arange(width, dtype=jnp.int32)
    core, y, zh, x, zl, r = digits(row, 2, 4, 2, 4, 2, width // 128)
    core = lax.rem(core + lax.axis_index("core"), 2)
    feature = ((((y * 2 + zh) * 4 + x) * 2 + core) * 2 + zl) * (width // 128) + r
    return (feature[:, None] == jnp.arange(width, dtype=jnp.int32)[None, :]).astype(BF)


def reduce_rows(keep, send):
    got = lax.ppermute(send, "core", [(0, 1), (1, 0)])
    joined = (keep.astype(F32) + got.astype(F32)).astype(BF)
    rows, columns = joined.shape
    parts = lax.all_to_all(joined.reshape(64, rows // 64, columns), CHIPS, 0, 0, tiled=True)
    return jnp.sum(parts.astype(F32), axis=0)


def on_device(layer_input, out_grad, slot_frame, ln_gain, ln_bias, w_qkv, w_out, time_bias):
    width = layer_input.shape[-1]
    frames = slot_frame.shape[1]
    rows_in = lax.all_to_all(split_patches(layer_input), SEQ, 0, 0, tiled=True)
    rows_grad = lax.all_to_all(split_patches(out_grad), SEQ, 0, 0, tiled=True)
    table = expand_bias(time_bias, frames)
    order = row_order(width)
    gain, bias = ln_gain.reshape(1, width), ln_bias.reshape(1, width)
    places, turned, proj, weights, att = forward(rows_in, gain, bias, w_qkv, table, order)
    grads, att_grad, val_grad, keep, send = values_backward(
        rows_grad, slot_frame, w_out, weights, att, turned, order
    )
    first_sums = reduce_rows(keep, send)
    pair, out_rows, sums = scores_backward(weights, proj, att_grad, val_grad, grads, places, w_qkv, gain)
    in_grad = merge_patches(lax.all_to_all(out_rows, SEQ, 0, 0, tiled=True))
    second_sums = reduce_rows(*pair_terms(turned, pair, order, sums))
    tokens = 128 * SPAN * frames
    scale = float(tokens) ** (-0.5)
    first_sums = first_sums * scale
    second_sums = second_sums * scale
    qkv_grad = jnp.concatenate([second_sums[:, : 2 * width], first_sums[:, :width]], axis=1)
    tail = second_sums[:, 2 * width :]
    return (in_grad, qkv_grad, first_sums[:, width:], tail[:, 0] + tail[:, 8], tail[:, 1] + tail[:, 9])


def solution(mesh):
    inner = Mesh(mesh.devices.reshape(4, 2, 4, 2, 2), ("y", "zh", "x", "core", "zl"))
    every = ("y", "zh", "x", "core", "zl")
    return jax.shard_map(
        on_device,
        mesh=inner,
        in_specs=(P("zl", SEQ, None, None), P("zl", SEQ, None, None), P("zl", None), P(), P(), P(), P(), P()),
        out_specs=(P("zl", SEQ, None, None), P(every, None), P(every, None), P(every), P(every)),
        check_vma=False,
    )
```

time: 1860 us -> 280 us (0.15)
  waiting for transfers between devices: 1150 us -> 92.2 us
  local copies, waits for them, and re-layouts: 405 us -> 5.67 us
  matrix products: 129 us -> 0 us
  Pallas kernels: 0 us -> 129 us
  blocking collectives: 83.7 us -> 0 us
  other arithmetic: 32.7 us -> 14 us
    reduce_scatter x2 -> x0, waiting for transfers between devices: 1150 us -> none  [the longest x1 658 us: on_device(): lax.psum_scatter(grad_terms[0], ('seq', 'rep'), scatter_dimension=0, tile...]
    gather x4 -> x0, local copies, waits for them, and re-layouts: 246 us -> none  [the longest x2 237 us: expand_bias(): return jnp.take(time_bias, offsets, axis=1)]
    dot_general x11 -> x0, matrix products: 129 us -> none  [the longest x1 23.9 us: position_backward(): jnp.einsum('phts,tphe->sphe', score_grad, queries, preferred_element_type...]
    pallas_call x0 -> x8, Pallas kernels: none -> 129 us  [the longest x1 40.7 us: forward(): pl.pallas_call(forward_kernel, grid=(SPAN,), in_specs=[full(rows.shape),...]
    all_to_all x3 -> x5, waiting for transfers between devices: 0.01 us -> 92.2 us  [the longest x2 50.6 us: reduce_rows(): lax.all_to_all(joined.reshape(64, rows // 64, columns), CHIPS, 0, 0, tile...]
    unnamed x1 -> x0, blocking collectives: 83.7 us -> none
    reshape x5 -> x1, local copies, waits for them, and re-layouts: 51.1 us -> 0.65 us  [expand_bias(): jnp.pad(time_bias[:, ::-1], ((0, 0), (0, 1))).reshape(heads, 1, 2 * frames)]
    unnamed x61 -> x10, local copies, waits for them, and re-layouts: 32.2 us -> 4.39 us
  transfers between devices with their start and end apart: 5 -> 7, of which waited for: 2 -> 4; matrix products, arithmetic and copies ran while one was open for 21% -> 5% of each run, Pallas kernels for 0% -> 37%
where the time goes in v1:
time: 280 us; the launch traced here: 279 us
  Pallas kernels  129 us (46%)
  waiting for transfers between devices  92.2 us (33%)
  starting transfers between devices  37.7 us (13%)
  other arithmetic  14 us (5%)
  local copies, waits for them, and re-layouts  5.67 us (2%)
    all_to_all x2, waiting for transfers between devices, reduce_rows(): lax.all_to_all(joined.reshape(64, rows // 64, columns), CHIPS, 0, 0, tile...  50.6 us
    pallas_call x1, Pallas kernels, forward(): pl.pallas_call(forward_kernel, grid=(SPAN,), in_specs=[full(rows.shape),...  40.7 us
    pallas_call x1, Pallas kernels, scores_backward(): pl.pallas_call(scores_kernel, grid=(SPAN,), in_specs=[per(heads, frames,...  34.7 us
    all_to_all x1, waiting for transfers between devices, on_device(): rows_in = lax.all_to_all(split_patches(layer_input), SEQ, 0, 0, tiled=True)  26.1 us
    pallas_call x1, Pallas kernels, values_backward(): pl.pallas_call(values_kernel, grid=(SPAN,), in_specs=[full(rows.shape), f...  20.6 us
    all_to_all x1, waiting for transfers between devices, on_device(): in_grad = merge_patches(lax.all_to_all(out_rows, SEQ, 0, 0, tiled=True))  15.5 us
    all_to_all x1, starting transfers between devices, on_device(): rows_in = lax.all_to_all(split_patches(layer_input), SEQ, 0, 0, tiled=True)  11.3 us
    all_to_all x2, starting transfers between devices, reduce_rows(): lax.all_to_all(joined.reshape(64, rows // 64, columns), CHIPS, 0, 0, tile...  10.7 us
  transfers between devices with their start and end apart: 7, of which 4 were waited for; matrix products, arithmetic and copies ran while one was open for 5% of the time, Pallas kernels for 37%

profile of v1, /device:TPU:0, one launch (start us, length us, event | category | flops | bytes accessed | tf_op | source)
XLA Modules:
  0.0 279.0 jit_solution(10521507219330008298)
XLA Ops:
  0.6 4.3 %split_patches.2 = bf16[64,16,1024]{2,1,0:T(8,128)(2,1)} custom-call(bf16[1,4,256,1024]{3,2,1,0:T(8,128)(2,1)} %rows_ref.2), custom_call_target="tpu_custom_call" | custom-call | flops 536870912 | bytes 4194304 | tf_op jit(solution)/shard_map/split_patches/pallas_call | solution.py:87
  5.0 11.3 %all-to-all-start = ((bf16[64,16,1024]{2,1,0:T(8,128)(2,1)}), bf16[64,16,1024]{2,1,0:T(8,128)(2,1)S(1)}, u32[]{:S(2)}, u32[]{:S(2)}) async-start(bf16[64,16,1024]{2,1,0:T(8,128)(2,1)} %split_patches.2), calls=%async_computation | async-start | bytes 4194304 | tf_op jit(solution)/shard_map/all_to_all | solution.py:435
  16.3 4.4 %split_patches.3 = bf16[64,16,1024]{2,1,0:T(8,128)(2,1)} custom-call(bf16[1,4,256,1024]{3,2,1,0:T(8,128)(2,1)} %rows_ref.3), custom_call_target="tpu_custom_call" | custom-call | flops 536870912 | bytes 4194304 | tf_op jit(solution)/shard_map/split_patches/pallas_call | solution.py:87
  20.7 0.0 copy-start.3
  20.7 26.1 %all-to-all-done.rows_ref = bf16[64,16,1024]{2,1,0:T(8,128)(2,1)S(1)} async-done(((bf16[64,16,1024]{2,1,0:T(8,128)(2,1)}), bf16[64,16,1024]{2,1,0:T(8,128)(2,1)S(1)}, u32[]{:S(2)}, u32[]{:S(2)}) %all-to-all-start) | async-done | bytes 2097184 | tf_op jit(solution)/shard_map/all_to_all | solution.py:435
  46.8 0.0 copy-start.2
  46.8 1.3 copy-done.2
  48.1 5.0 %all-to-all-start.1 = ((bf16[64,16,1024]{2,1,0:T(8,128)(2,1)}), bf16[64,16,1024]{2,1,0:T(8,128)(2,1)S(1)}, u32[]{:S(2)}, u32[]{:S(2)}) async-start(bf16[64,16,1024]{2,1,0:T(8,128)(2,1)} %split_patches.3), calls=%async_computation.1 | async-start | bytes 4194304 | tf_op jit(solution)/shard_map/all_to_all | solution.py:436
  53.2 0.0 copy-done.3
  53.2 0.3 reverse
  53.5 0.1 slice.48
  53.6 0.6 reshape.94.bias_ref
  54.2 9.1 %expand_bias.1.table_ref = f32[16,256,256]{2,1,0:T(8,128)} custom-call(f32[16,1,512]{2,1,0:T(1,128)} %reshape.94.bias_ref), custom_call_target="tpu_custom_call" | custom-call | flops 8388608 | bytes 4194304 | tf_op jit(solution)/shard_map/expand_bias/pallas_call | solution.py:128
  63.4 1.7 fusion.order_ref
  65.1 40.7 %forward.1 = (bf16[4,256,1024]{2,1,0:T(8,128)(2,1)}, bf16[1024,1024]{1,0:T(8,128)(2,1)}, bf16[4,256,3072]{2,1,0:T(8,128)(2,1)}, bf16[4,16,256,256]{3,2,1,0:T(8,128)(2,1)}, bf16[4,256,1024]{2,1,0:T(8,128)(2,1)}) custom-call(bf16[64,16,1024]{2,1,0:T(8,128)(2,1)} %copy-done.2, f32[1,1024]{1,0:T(1,128)} %bitcast.9, f32[1,1024]{1,0:T(1,128)} %bitcast.8, ...), custom_call_target="tpu_custom_call" | custom-call | flops 16000000000 | bytes 35651584 | tf_op jit(solution)/shard_map/forward/pallas_call | solution.py:208
  105.8 0.0 all-to-all-done.1.rows_ref
  105.8 0.0 copy-start.1
  105.8 1.3 copy-done.1
  107.1 20.6 %values_backward.1 = (bf16[4,256,1024]{2,1,0:T(8,128)(2,1)}, bf16[4,256,1024]{2,1,0:T(8,128)(2,1)}, bf16[4,256,1024]{2,1,0:T(8,128)(2,1)}, bf16[512,2048]{1,0:T(8,128)(2,1)}, bf16[512,2048]{1,0:T(8,128)(2,1)}) custom-call(bf16[64,16,1024]{2,1,0:T(8,128)(2,1)} %copy-done.1, s32[1,256]{1,0:T(1,128)} %slot_ref.1, bf16[1024,1024]{1,0:T(8,128)(2,1)} %w_ref.4, ...), custom_call_target="tpu_custom_call" | custom-call | flops 12000000000 | bytes 29360128 | tf_op jit(solution)/shard_map/values_backward/pallas_call | solution.py:284
  127.8 0.1 collective-permute-start.1
  127.9 34.7 %scores_backward.1 = (bf16[4,256,2048]{2,1,0:T(8,128)(2,1)}, bf16[64,16,1024]{2,1,0:T(8,128)(2,1)}, f32[8,1024]{1,0:T(8,128)}) custom-call(bf16[4,16,256,256]{3,2,1,0:T(8,128)(2,1)} %get-tuple-element.20.weights_ref, bf16[4,256,3072]{2,1,0:T(8,128)(2,1)} %get-tuple-element.21.proj_ref, bf16[4,256,1024]{2,1,0:T(8,128)(2,1)} %get-tuple-element.24.att_grad_ref, ...), custom_call_target="tpu_custom_call" | custom-call | flops 17999998976 | bytes 35651584 | tf_op jit(solution)/shard_map/scores_backward/pallas_call | solution.py:364
  162.6 10.4 %all-to-all-start.2 = ((bf16[64,16,1024]{2,1,0:T(8,128)(2,1)}), bf16[64,16,1024]{2,1,0:T(8,128)(2,1)S(1)}, u32[]{:S(2)}, u32[]{:S(2)}) async-start(bf16[64,16,1024]{2,1,0:T(8,128)(2,1)} %get-tuple-element.28), calls=%async_computation.2 | async-start | bytes 4194304 | tf_op jit(solution)/shard_map/all_to_all | solution.py:446
  173.1 10.4 %pair_terms.1 = (bf16[512,2176]{1,0:T(8,128)(2,1)}, bf16[512,2176]{1,0:T(8,128)(2,1)}) custom-call(bf16[1024,1024]{1,0:T(8,128)(2,1)} %get-tuple-element.23.turned_ref, bf16[4,256,2048]{2,1,0:T(8,128)(2,1)} %get-tuple-element.29.pair_ref, bf16[1024,1024]{1,0:T(8,128)(2,1)} %fusion.order_ref, f32[8,1024]{1,0:T(8,128)} %get-tuple-element.30.sums_ref), custom_call_target="tpu_custom_call" | custom-call | flops 4294967296 | bytes 14680064 | tf_op jit(solution)/shard_map/pair_terms/pallas_call | solution.py:407
  183.5 0.1 collective-permute-start
  183.5 0.0 collective-permute-done.1
  183.6 4.5 %fusion.2 = bf16[64,8,2048]{2,1,0:T(8,128)(2,1)} fusion(bf16[512,2048]{1,0:T(8,128)(2,1)} %collective-permute-done.1, bf16[512,2048]{1,0:T(8,128)(2,1)} %get-tuple-element.33), kind=kLoop, calls=%fused_computation.7 | loop fusion | flops 4194304 | bytes 6291456 | tf_op jit(solution)/shard_map/reshape | solution.py:428
  188.0 15.5 %all-to-all-done.2.rows_ref = bf16[64,16,1024]{2,1,0:T(8,128)(2,1)S(1)} async-done(((bf16[64,16,1024]{2,1,0:T(8,128)(2,1)}), bf16[64,16,1024]{2,1,0:T(8,128)(2,1)S(1)}, u32[]{:S(2)}, u32[]{:S(2)}) %all-to-all-start.2) | async-done | bytes 2097184 | tf_op jit(solution)/shard_map/all_to_all | solution.py:446
  203.6 0.0 copy-start
  203.6 1.4 copy-done
  204.9 5.8 %all-to-all-start.4 = ((bf16[64,8,2048]{2,1,0:T(8,128)(2,1)}), bf16[64,8,2048]{2,1,0:T(8,128)(2,1)}, u32[]{:S(2)}, u32[]{:S(2)}) async-start(bf16[64,8,2048]{2,1,0:T(8,128)(2,1)} %fusion.2), calls=%async_computation.4 | async-start | bytes 4194304 | tf_op jit(solution)/shard_map/all_to_all | solution.py:428
  210.7 0.0 collective-permute-done
  210.7 4.2 %fusion.1 = bf16[64,8,2176]{2,1,0:T(8,128)(2,1)} fusion(bf16[512,2176]{1,0:T(8,128)(2,1)} %collective-permute-done, bf16[512,2176]{1,0:T(8,128)(2,1)} %get-tuple-element.31), kind=kLoop, calls=%fused_computation.6 | loop fusion | flops 4456448 | bytes 6684672 | tf_op jit(solution)/shard_map/reshape | solution.py:428
  214.9 26.5 %all-to-all-done.4 = bf16[64,8,2048]{2,1,0:T(8,128)(2,1)} async-done(((bf16[64,8,2048]{2,1,0:T(8,128)(2,1)}), bf16[64,8,2048]{2,1,0:T(8,128)(2,1)}, u32[]{:S(2)}, u32[]{:S(2)}) %all-to-all-start.4) | async-done | bytes 2097184 | tf_op jit(solution)/shard_map/all_to_all | solution.py:428
  241.4 4.9 %all-to-all-start.3 = ((bf16[64,8,2176]{2,1,0:T(8,128)(2,1)}), bf16[64,8,2176]{2,1,0:T(8,128)(2,1)S(1)}, u32[]{:S(2)}, u32[]{:S(2)}) async-start(bf16[64,8,2176]{2,1,0:T(8,128)(2,1)} %fusion.1), calls=%async_computation.3 | async-start | bytes 4456448 | tf_op jit(solution)/shard_map/all_to_all | solution.py:428
  246.3 4.3 %merge_patches.1 = bf16[1,4,256,1024]{3,2,1,0:T(8,128)(2,1)} custom-call(bf16[64,16,1024]{2,1,0:T(8,128)(2,1)} %copy-done), custom_call_target="tpu_custom_call" | custom-call | flops 536870912 | bytes 4194304 | tf_op jit(solution)/shard_map/merge_patches/pallas_call | solution.py:106
  250.6 1.9 convert_reduce_fusion.1
  252.5 0.6 fusion.21
  253.2 24.1 %all-to-all-done.3 = bf16[64,8,2176]{2,1,0:T(8,128)(2,1)S(1)} async-done(((bf16[64,8,2176]{2,1,0:T(8,128)(2,1)}), bf16[64,8,2176]{2,1,0:T(8,128)(2,1)S(1)}, u32[]{:S(2)}, u32[]{:S(2)}) %all-to-all-start.3) | async-done | bytes 2228256 | tf_op jit(solution)/shard_map/all_to_all | solution.py:428
  277.3 0.3 convert_reduce_fusion
  277.6 0.7 fusion.16
  278.3 0.6 pad_maximum_fusion
  (5 shorter events, 0.1 us)
Async XLA Ops:
  5.0 41.8 %all-to-all-start = ((bf16[64,16,1024]{2,1,0:T(8,128)(2,1)}), bf16[64,16,1024]{2,1,0:T(8,128)(2,1)S(1)}, u32[]{:S(2)}, u32[]{:S(2)}) async-start(bf16[64,16,1024]{2,1,0:T(8,128)(2,1)} %split_patches.2), calls=%async_computation | async-start | bytes 4194304 | tf_op jit(solution)/shard_map/all_to_all | solution.py:435
  20.7 32.4 %copy-start.3 = (f32[16,511]{1,0:T(8,128)S(1)}, f32[16,511]{1,0:T(8,128)}, u32[]{:S(2)}) copy-start(f32[16,511]{1,0:T(8,128)} %param.15) | copy-start | bytes 98116
  46.8 1.3 copy-start.2
  48.1 57.7 %all-to-all-start.1 = ((bf16[64,16,1024]{2,1,0:T(8,128)(2,1)}), bf16[64,16,1024]{2,1,0:T(8,128)(2,1)S(1)}, u32[]{:S(2)}, u32[]{:S(2)}) async-start(bf16[64,16,1024]{2,1,0:T(8,128)(2,1)} %split_patches.3), calls=%async_computation.1 | async-start | bytes 4194304 | tf_op jit(solution)/shard_map/all_to_all | solution.py:436
  105.8 1.3 copy-start.1
  127.8 55.8 %collective-permute-start.1 = (bf16[512,2048]{1,0:T(8,128)(2,1)}, bf16[512,2048]{1,0:T(8,128)(2,1)}, u32[]{:S(2)}, u32[]{:S(2)}) collective-permute-start(bf16[512,2048]{1,0:T(8,128)(2,1)} %get-tuple-element.34), channel_id=1, source_target_pairs={{0,2},{2,0},{1,3},{3,1},{4,6},{6,4},{5,7},{7,5},{8,10},{10,8},{9,1... | collective-permute-start | bytes 6291464 | tf_op jit(solution)/shard_map/ppermute | solution.py:425
  162.6 40.9 %all-to-all-start.2 = ((bf16[64,16,1024]{2,1,0:T(8,128)(2,1)}), bf16[64,16,1024]{2,1,0:T(8,128)(2,1)S(1)}, u32[]{:S(2)}, u32[]{:S(2)}) async-start(bf16[64,16,1024]{2,1,0:T(8,128)(2,1)} %get-tuple-element.28), calls=%async_computation.2 | async-start | bytes 4194304 | tf_op jit(solution)/shard_map/all_to_all | solution.py:446
  183.5 27.2 %collective-permute-start = (bf16[512,2176]{1,0:T(8,128)(2,1)}, bf16[512,2176]{1,0:T(8,128)(2,1)}, u32[]{:S(2)}, u32[]{:S(2)}) collective-permute-start(bf16[512,2176]{1,0:T(8,128)(2,1)} %get-tuple-element.32), channel_id=1, source_target_pairs={{0,2},{2,0},{1,3},{3,1},{4,6},{6,4},{5,7},{7,5},{8,10},{10,8},{9,1... | collective-permute-start | bytes 6684680 | tf_op jit(solution)/shard_map/ppermute | solution.py:425
  203.6 1.4 copy-start
  204.9 36.4 %all-to-all-start.4 = ((bf16[64,8,2048]{2,1,0:T(8,128)(2,1)}), bf16[64,8,2048]{2,1,0:T(8,128)(2,1)}, u32[]{:S(2)}, u32[]{:S(2)}) async-start(bf16[64,8,2048]{2,1,0:T(8,128)(2,1)} %fusion.2), calls=%async_computation.4 | async-start | bytes 4194304 | tf_op jit(solution)/shard_map/all_to_all | solution.py:428
  241.4 35.9 %all-to-all-start.3 = ((bf16[64,8,2176]{2,1,0:T(8,128)(2,1)}), bf16[64,8,2176]{2,1,0:T(8,128)(2,1)S(1)}, u32[]{:S(2)}, u32[]{:S(2)}) async-start(bf16[64,8,2176]{2,1,0:T(8,128)(2,1)} %fusion.1), calls=%async_computation.3 | async-start | bytes 4456448 | tf_op jit(solution)/shard_map/all_to_all | solution.py:428

commit v2 on v1

v2 whole, which is shorter than its diff:
```python
import functools

import jax
import jax.numpy as jnp
from jax import lax
from jax.experimental import pallas as pl
from jax.experimental.pallas import tpu as pltpu
from jax.sharding import Mesh, PartitionSpec as P

BF = jnp.bfloat16
F32 = jnp.float32
VMEM_BYTES = 36 * 1024 * 1024
SCORES_VMEM = 60 * 1024 * 1024
SPAN = 4
GROUP = 16
PAIR = 128
SEQ = ("y", "zh", "x", "core")
CHIPS = ("y", "zh", "x", "zl")
PLANE = ("y", "zh", "zl")

NT = (((1,), (1,)), ((), ()))
TN = (((0,), (0,)), ((), ()))


def mm(a, b, dims=(((1,), (0,)), ((), ()))):
    return lax.dot_general(a, b, dims, preferred_element_type=F32)


def params(*semantics):
    return pltpu.CompilerParams(vmem_limit_bytes=VMEM_BYTES)


def cost(flops, moved, transcendentals=0):
    return pl.CostEstimate(flops=flops, bytes_accessed=moved, transcendentals=transcendentals)


def full(shape):
    return pl.BlockSpec(shape, lambda *ids: (0,) * len(shape), pipeline_mode=pl.Buffered(1))


def digits(index, *sizes):
    out = []
    for size in reversed(sizes):
        out.append(lax.rem(index, size))
        index = lax.div(index, size)
    return out[::-1]


def one_hot_rows(targets, shape, axis):
    return (targets == lax.broadcasted_iota(jnp.int32, shape, axis)).astype(F32).astype(BF)


def frame_major_from(shape):
    row = lax.broadcasted_iota(jnp.int32, shape, 0)
    block, place, frame = digits(row, GROUP, SPAN, SPAN)
    return one_hot_rows((frame * GROUP + block) * SPAN + place, shape, 1)


def frame_major_to(shape):
    col = lax.broadcasted_iota(jnp.int32, shape, 1)
    block, place, frame = digits(col, GROUP, SPAN, SPAN)
    return one_hot_rows((frame * GROUP + block) * SPAN + place, shape, 0)


def place_major_from(shape):
    col = lax.broadcasted_iota(jnp.int32, shape, 1)
    block, place, frame = digits(col, GROUP, SPAN, SPAN)
    return one_hot_rows((place * GROUP + block) * SPAN + frame, shape, 0)


def place_major_to(shape):
    row = lax.broadcasted_iota(jnp.int32, shape, 0)
    block, place, frame = digits(row, GROUP, SPAN, SPAN)
    return one_hot_rows((place * GROUP + block) * SPAN + frame, shape, 1)


SQUARE = (GROUP * SPAN * SPAN, GROUP * SPAN * SPAN)


def split_kernel(rows_ref, out_ref):
    spread = rows_ref[0].reshape(SQUARE[0], rows_ref.shape[-1])
    moved = mm(frame_major_from(SQUARE), spread).astype(BF)
    out_ref[...] = moved.reshape(out_ref.shape)


def split_patches(rows):
    _, span, patches, width = rows.shape
    blocks = patches // span
    return pl.pallas_call(
        split_kernel,
        grid=(blocks // GROUP,),
        in_specs=[pl.BlockSpec((1, span, GROUP * span, width), lambda c: (0, 0, c, 0))],
        out_specs=pl.BlockSpec((GROUP, span * span, width), lambda c: (c, 0, 0)),
        out_shape=jax.ShapeDtypeStruct((blocks, span * span, width), BF),
        compiler_params=params(),
        cost_estimate=cost(2 * 256 * rows.size, 4 * rows.size),
        name="split_patches",
    )(rows)


def merge_kernel(rows_ref, out_ref):
    moved = mm(frame_major_to(SQUARE), rows_ref[...].reshape(SQUARE[0], rows_ref.shape[-1]))
    out_ref[0] = moved.astype(BF).reshape(out_ref.shape[1:])


def merge_patches(rows):
    blocks, rows_each, width = rows.shape
    return pl.pallas_call(
        merge_kernel,
        grid=(blocks // GROUP,),
        in_specs=[pl.BlockSpec((GROUP, rows_each, width), lambda c: (c, 0, 0))],
        out_specs=pl.BlockSpec((1, SPAN, GROUP * SPAN, width), lambda c: (0, 0, c, 0)),
        out_shape=jax.ShapeDtypeStruct((1, SPAN, blocks * SPAN, width), BF),
        compiler_params=params(),
        cost_estimate=cost(2 * 256 * rows.size, 4 * rows.size),
        name="merge_patches",
    )(rows)


def prepare_kernel(rows_ref, bias_ref, out_ref, table_ref):
    split_kernel(rows_ref, out_ref)
    heads, frames, _ = table_ref.shape
    for h in range(heads):
        wide = jnp.broadcast_to(bias_ref[h], (frames, 2 * frames))
        table_ref[h] = pltpu.roll(wide, frames + 1, 1, stride=1, stride_axis=0)[:, :frames]


def prepare(rows, time_bias, frames):
    _, span, patches, width = rows.shape
    blocks = patches // span
    steps = blocks // GROUP
    heads = time_bias.shape[0]
    turned = jnp.pad(time_bias[:, ::-1], ((0, 0), (0, 1))).reshape(heads, 1, 2 * frames)
    return pl.pallas_call(
        prepare_kernel,
        grid=(steps,),
        in_specs=[
            pl.BlockSpec((1, span, GROUP * span, width), lambda c: (0, 0, c, 0)),
            pl.BlockSpec((heads // steps, 1, 2 * frames), lambda c: (c, 0, 0)),
        ],
        out_specs=[
            pl.BlockSpec((GROUP, span * span, width), lambda c: (c, 0, 0)),
            pl.BlockSpec((heads // steps, frames, frames), lambda c: (c, 0, 0)),
        ],
        out_shape=[
            jax.ShapeDtypeStruct((blocks, span * span, width), BF),
            jax.ShapeDtypeStruct((heads, frames, frames), F32),
        ],
        compiler_params=params(),
        cost_estimate=cost(2 * 256 * rows.size, 4 * rows.size + 4 * 2**20),
        name="prepare",
    )(rows, turned)


def gather_places(rows_ref, out_ref):
    blocks, _, width = rows_ref.shape
    order = place_major_from(SQUARE)
    run = GROUP * SPAN
    for c in range(blocks // GROUP):
        chunk = rows_ref[c * GROUP : (c + 1) * GROUP].reshape(SQUARE[0], width)
        moved = mm(order, chunk).astype(BF)
        for p in range(SPAN):
            out_ref[p, c * run : (c + 1) * run, :] = moved[p * run : (p + 1) * run, :]


def norm_parts(values):
    mean = jnp.mean(values, axis=-1, keepdims=True)
    centred = values - mean
    inv_std = lax.rsqrt(jnp.mean(centred * centred, axis=-1, keepdims=True) + 1e-05)
    return centred * inv_std, inv_std


def halves(frames):
    return lax.broadcasted_iota(jnp.int32, (frames, PAIR), 1) < PAIR // 2


def forward_kernel(
    rows_ref, gain_ref, bias_ref, w_ref, table_ref,
    places_ref, turned_ref, proj_ref, weights_ref, att_ref, places,
):
    step = pl.program_id(0)

    @pl.when(step == 0)
    def _():
        gather_places(rows_ref, places)

    rows = places[step]
    places_ref[0] = rows
    normed, _ = norm_parts(rows.astype(F32))
    hidden = (normed * gain_ref[...] + bias_ref[...]).astype(BF)
    turned_ref[...] = hidden.T
    width = hidden.shape[1]
    factor = 0.125
    proj_ref[0, :, :width] = (mm(hidden, w_ref[:, :width]) * factor).astype(BF)
    proj_ref[0, :, width : 2 * width] = mm(hidden, w_ref[:, width : 2 * width]).astype(BF)
    proj_ref[0, :, 2 * width :] = mm(hidden, w_ref[:, 2 * width :]).astype(BF)
    frames = rows.shape[0]
    first = halves(frames)
    for i in range(width // PAIR):
        lanes = slice(i * PAIR, (i + 1) * PAIR)
        queries = proj_ref[0, :, lanes]
        keys = proj_ref[0, :, width + i * PAIR : width + (i + 1) * PAIR]
        vals = proj_ref[0, :, 2 * width + i * PAIR : 2 * width + (i + 1) * PAIR]
        parts = []
        for h in range(2):
            mine = jnp.where(first if h == 0 else ~first, keys, jnp.zeros_like(keys))
            scores = mm(mine, queries, NT) + table_ref[2 * i + h]
            top = jnp.max(scores, axis=0, keepdims=True)
            raised = jnp.exp(scores - top)
            total = jnp.sum(raised, axis=0, keepdims=True)
            short = (raised * (1.0 / total)).astype(BF)
            weights_ref[0, 2 * i + h] = short
            parts.append(mm(short, vals, TN))
        att_ref[0, :, lanes] = jnp.where(first, parts[0], parts[1]).astype(BF)


def forward(rows, gain, bias, w_qkv, table):
    blocks, _, width = rows.shape
    frames = blocks * SPAN
    heads = table.shape[0]
    per = lambda *tail: pl.BlockSpec((1,) + tail, lambda p: (p,) + (0,) * len(tail))
    return pl.pallas_call(
        forward_kernel,
        grid=(SPAN,),
        in_specs=[full(rows.shape), full((1, width)), full((1, width)), full(w_qkv.shape),
                  full(table.shape)],
        out_specs=[
            per(frames, width),
            pl.BlockSpec((width, frames), lambda p: (0, p)),
            per(frames, 3 * width),
            per(heads, frames, frames),
            per(frames, width),
        ],
        out_shape=[
            jax.ShapeDtypeStruct((SPAN, frames, width), BF),
            jax.ShapeDtypeStruct((width, SPAN * frames), BF),
            jax.ShapeDtypeStruct((SPAN, frames, 3 * width), BF),
            jax.ShapeDtypeStruct((SPAN, heads, frames, frames), BF),
            jax.ShapeDtypeStruct((SPAN, frames, width), BF),
        ],
        scratch_shapes=[pltpu.VMEM((SPAN, frames, width), BF)],
        compiler_params=params(),
        cost_estimate=cost(16 * 10**9, 34 * 2**20, 2**22),
        name="forward",
    )(rows, gain, bias, w_qkv, table)


def place_rows(terms, order_ref, line, keep_ref, send_ref, cols):
    count = order_ref.shape[1]
    half = count // 2
    for i in range(0, count, 2):
        pair = []
        for j in (i, i + 1):
            start = pl.multiple_of(order_ref[line, j] * 8, 8)
            pair.append(terms[pl.ds(start, 8), :])
        rows = jnp.concatenate(pair, axis=0).astype(BF)
        target, at = (keep_ref, i) if i < half else (send_ref, i - half)
        target[at * 8 : at * 8 + 16, cols] = rows


def values_kernel(
    order_ref, rows_ref, slot_ref, w_ref, weights_ref, att_ref, turned_ref,
    grad_ref, att_grad_ref, val_grad_ref, keep_ref, send_ref, places, turned_grad, val_grads, terms,
):
    step = pl.program_id(0)

    @pl.when(step == 0)
    def _():
        gather_places(rows_ref, places)

    frames, width = places.shape[1:]
    natural = one_hot_rows(slot_ref[...], (frames, frames), 0)
    grads = mm(natural, places[step]).astype(BF)
    grad_ref[0] = grads
    here = pl.ds(pl.multiple_of(step * frames, frames), frames)
    turned_grad[:, here] = grads.T
    att_grad_ref[0] = mm(grads, w_ref[...], NT).astype(BF)
    first = halves(frames)
    for i in range(width // PAIR):
        lanes = slice(i * PAIR, (i + 1) * PAIR)
        att_grad = att_grad_ref[0, :, lanes]
        parts = [mm(weights_ref[0, 2 * i + h], att_grad) for h in range(2)]
        merged = jnp.where(first, parts[0], parts[1]).astype(BF)
        val_grad_ref[0, :, lanes] = merged
        val_grads[here, lanes] = merged

    @pl.when(step == pl.num_programs(0) - 1)
    def _():
        chunk = terms.shape[1]
        for c in range(width // chunk):
            cols = slice(c * chunk, (c + 1) * chunk)
            after = slice(width + c * chunk, width + (c + 1) * chunk)
            terms[...] = mm(turned_ref[...], val_grads[:, cols])
            place_rows(terms, order_ref, 0, keep_ref, send_ref, cols)
            terms[...] = mm(turned_grad[...], att_ref[:, :, cols].reshape(SPAN * frames, chunk))
            place_rows(terms, order_ref, 0, keep_ref, send_ref, after)


def values_backward(order, rows, slot_frame, w_out, weights, att, turned):
    blocks, _, width = rows.shape
    frames = blocks * SPAN
    heads = weights.shape[1]
    tokens = SPAN * frames
    per = lambda *tail: pl.BlockSpec((1,) + tail, lambda p, _: (p,) + (0,) * len(tail))
    rows_each = jax.ShapeDtypeStruct((SPAN, frames, width), BF)
    half = jax.ShapeDtypeStruct((width // 2, 2 * width), BF)
    return pl.pallas_call(
        values_kernel,
        grid_spec=pltpu.PrefetchScalarGridSpec(
            num_scalar_prefetch=1,
            grid=(SPAN,),
            in_specs=[full(rows.shape), full(slot_frame.shape), full(w_out.shape), per(heads, frames, frames),
                      full(att.shape), full(turned.shape)],
            out_specs=[per(frames, width), per(frames, width), per(frames, width), full(half.shape), full(half.shape)],
            scratch_shapes=[
                pltpu.VMEM((SPAN, frames, width), BF),
                pltpu.VMEM((width, tokens), BF),
                pltpu.VMEM((tokens, width), BF),
                pltpu.VMEM((width, 256), F32),
            ],
        ),
        out_shape=[rows_each, rows_each, rows_each, half, half],
        compiler_params=params(),
        cost_estimate=cost(12 * 10**9, 28 * 2**20),
        name="values_backward",
    )(order, rows, slot_frame, w_out, weights, att, turned)


def scores_kernel(
    order_ref, joined_ref, weights_ref, proj_ref, att_grad_ref, val_grad_ref, grad_ref, places_ref, w_ref, gain_ref,
    turned_ref, out_ref, keep_ref, send_ref, results, pairs, sums, terms,
):
    step = pl.program_id(0)
    frames, width = grad_ref.shape[1:]
    first = halves(frames)
    factor = 0.125
    here = pl.ds(pl.multiple_of(step * frames, frames), frames)
    for i in range(width // PAIR):
        lanes = slice(i * PAIR, (i + 1) * PAIR)
        key_lanes = slice(width + i * PAIR, width + (i + 1) * PAIR)
        queries = proj_ref[0, :, lanes]
        keys = proj_ref[0, :, key_lanes]
        vals = proj_ref[0, :, 2 * width + i * PAIR : 2 * width + (i + 1) * PAIR]
        att_grad = att_grad_ref[0, :, lanes]
        key_parts, query_parts = [], []
        for h in range(2):
            mine = jnp.where(first if h == 0 else ~first, vals, jnp.zeros_like(vals))
            weight_grad = mm(mine, att_grad, NT)
            weights = weights_ref[0, 2 * i + h].astype(F32)
            shared = jnp.sum(weight_grad * weights, axis=0, keepdims=True)
            score_grad = (weights * (weight_grad - shared)).astype(BF)
            key_parts.append(mm(score_grad, queries))
            query_parts.append(mm(score_grad, keys, TN))
        pairs[here, lanes] = (jnp.where(first, query_parts[0], query_parts[1]) * factor).astype(BF)
        pairs[here, key_lanes] = jnp.where(first, key_parts[0], key_parts[1]).astype(BF)

    hidden_grad = mm(pairs[here, :], w_ref[:, : 2 * width], NT) + mm(val_grad_ref[0], w_ref[:, 2 * width :], NT)
    normed, inv_std = norm_parts(places_ref[0].astype(F32))
    scaled = hidden_grad * gain_ref[...]
    norm_grad = inv_std * (
        scaled
        - jnp.mean(scaled, axis=-1, keepdims=True)
        - normed * jnp.mean(scaled * normed, axis=-1, keepdims=True)
    )
    results[step] = (grad_ref[0].astype(F32) + norm_grad).astype(BF)
    gain_term = jnp.sum(hidden_grad * normed, axis=0, keepdims=True)
    bias_term = jnp.sum(hidden_grad, axis=0, keepdims=True)

    @pl.when(step == 0)
    def _():
        sums[...] = jnp.zeros_like(sums)

    sums[0:1, :] += gain_term
    sums[1:2, :] += bias_term

    @pl.when(step == pl.num_programs(0) - 1)
    def _():
        order = place_major_to(SQUARE)
        run = GROUP * SPAN
        for c in range(frames // run):
            chunk = results[:, c * run : (c + 1) * run, :].reshape(SQUARE[0], width)
            moved = mm(order, chunk).astype(BF)
            out_ref[c * GROUP : (c + 1) * GROUP] = moved.reshape(GROUP, SPAN * SPAN, width)
        chunk = terms.shape[1]
        for at in range(0, 2 * width, chunk):
            terms[...] = mm(turned_ref[...], pairs[:, at : at + chunk])
            place_rows(terms, order_ref, 1, keep_ref, send_ref, slice(at, at + chunk))
        terms[:, :PAIR] = jnp.concatenate([sums[...]] * (PAIR // sums.shape[0]), axis=0).T
        place_rows(terms.at[:, :PAIR], order_ref, 1, keep_ref, send_ref, slice(2 * width, 2 * width + PAIR))


def scores_backward(order, joined, weights, proj, att_grad, val_grad, grads, places, w_qkv, gain, turned):
    _, frames, width = grads.shape
    heads = weights.shape[1]
    blocks = frames // SPAN
    tokens = SPAN * frames
    per = lambda *tail: pl.BlockSpec((1,) + tail, lambda p, _: (p,) + (0,) * len(tail))
    half = jax.ShapeDtypeStruct((width // 2, 2 * width + PAIR), BF)
    outs = [jax.ShapeDtypeStruct((blocks, SPAN * SPAN, width), BF), half, half]
    return pl.pallas_call(
        scores_kernel,
        grid_spec=pltpu.PrefetchScalarGridSpec(
            num_scalar_prefetch=1,
            grid=(SPAN,),
            in_specs=[pl.BlockSpec(memory_space=pl.ANY), per(heads, frames, frames), per(frames, 3 * width),
                      per(frames, width), per(frames, width), per(frames, width), per(frames, width),
                      full(w_qkv.shape), full((1, width)), full(turned.shape)],
            out_specs=[full(o.shape) for o in outs],
            scratch_shapes=[
                pltpu.VMEM((SPAN, frames, width), BF),
                pltpu.VMEM((tokens, 2 * width), BF),
                pltpu.VMEM((8, width), F32),
                pltpu.VMEM((width, 256), F32),
            ],
        ),
        out_shape=outs,
        compiler_params=pltpu.CompilerParams(vmem_limit_bytes=SCORES_VMEM),
        cost_estimate=cost(24 * 10**9, 34 * 2**20),
        name="scores_backward",
    )(order, joined, weights, proj, att_grad, val_grad, grads, places, w_qkv, gain, turned)


def total_kernel(parts_ref, *refs):
    total_ref = refs[len(refs) // 2]
    total_ref[...] = jnp.sum(parts_ref[...].astype(F32), axis=0)


def sum_parts(parts, *passed):
    anywhere = [pl.BlockSpec(memory_space=pltpu.HBM)] * len(passed)
    here = pl.BlockSpec(memory_space=pltpu.VMEM)
    return pl.pallas_call(
        total_kernel,
        in_specs=[here] + anywhere,
        out_specs=[here] + anywhere,
        out_shape=[jax.ShapeDtypeStruct(parts.shape[1:], F32)]
        + [jax.ShapeDtypeStruct(p.shape, p.dtype) for p in passed],
        input_output_aliases={i + 1: i + 1 for i in range(len(passed))},
        compiler_params=params(),
        cost_estimate=cost(parts.size, 2 * parts.size),
        name="sum_parts",
    )(parts, *passed)


def gray(place):
    return place ^ (place >> 1)


def row_orders():
    place = jnp.arange(128, dtype=jnp.int32)
    core = lax.axis_index("core") ^ (place >> 6)

    def block(y, zh, x, zl):
        return (((y * 2 + zh) * 4 + x) * 2 + core) * 2 + zl

    direct = block(*digits(place & 63, 4, 2, 4, 2))
    one, two, y, zh, zl = digits(place & 63, 2, 2, 4, 2, 2)
    mask = jnp.where(core == 0, one + 2 * two, 2 * one + two)
    x = gray(gray(lax.axis_index("x")) ^ mask)
    return jnp.stack([direct, block(y, zh, x, zl)]).astype(jnp.int32)


def neighbours(step):
    pairs = []
    for place in range(4):
        for core in range(2):
            mask = 1 if step == core else 2
            pairs.append((place * 2 + core, gray(gray(place) ^ mask) * 2 + core))
    return pairs


def after_kernel(held_ref, other_ref, out_ref):
    del held_ref, other_ref, out_ref


def after(held, other):
    anywhere = pl.BlockSpec(memory_space=pltpu.HBM)
    return pl.pallas_call(
        after_kernel,
        in_specs=[anywhere, anywhere],
        out_specs=anywhere,
        out_shape=jax.ShapeDtypeStruct(held.shape, held.dtype),
        input_output_aliases={0: 0},
        name="after",
    )(held, other)


def add(a, b):
    return (a.astype(F32) + b.astype(F32)).astype(BF)


def halve(held, step):
    half = held.shape[0] // 2
    return add(held[:half], lax.ppermute(held[half:], ("x", "core"), neighbours(step)))


def join_cores(keep, send):
    return add(keep, lax.ppermute(send, "core", [(0, 1), (1, 0)]))


def to_owners(joined, axes, count):
    rows, columns = joined.shape
    return lax.all_to_all(joined.reshape(count, rows // count, columns), axes, 0, 0, tiled=True)


def on_device(layer_input, out_grad, slot_frame, ln_gain, ln_bias, w_qkv, w_out, time_bias):
    width = layer_input.shape[-1]
    frames = slot_frame.shape[1]
    rows_in = lax.all_to_all(split_patches(layer_input), SEQ, 0, 0, tiled=True)
    split_grad, table = prepare(out_grad, time_bias, frames)
    rows_grad = lax.all_to_all(split_grad, SEQ, 0, 0, tiled=True)
    orders = row_orders()
    gain, bias = ln_gain.reshape(1, width), ln_bias.reshape(1, width)
    places, turned, proj, weights, att = forward(rows_in, gain, bias, w_qkv, table)
    grads, att_grad, val_grad, keep, send = values_backward(
        orders, rows_grad, slot_frame, w_out, weights, att, turned
    )
    joined = join_cores(keep, send)
    parts = to_owners(joined, CHIPS, 64)
    out_rows, keep, send = scores_backward(
        orders, joined, weights, proj, att_grad, val_grad, grads, places, w_qkv, gain, turned
    )
    first_sums, out_rows, keep, send = sum_parts(parts, out_rows, keep, send)
    out_parts = lax.all_to_all(out_rows, SEQ, 0, 0, tiled=True)
    held = halve(halve(join_cores(keep, send), 0), 1)
    in_grad = merge_patches(out_parts)
    held = after(held, out_parts)
    second_sums = jnp.sum(to_owners(held, PLANE, 16).astype(F32), axis=0)
    tokens = 128 * SPAN * frames
    scale = float(tokens) ** (-0.5)
    first_sums = first_sums * scale
    second_sums = second_sums * scale
    qkv_grad = jnp.concatenate([second_sums[:, : 2 * width], first_sums[:, :width]], axis=1)
    tail = second_sums[:, 2 * width :]
    return (in_grad, qkv_grad, first_sums[:, width:], tail[:, 0], tail[:, 1])


def solution(mesh):
    inner = Mesh(mesh.devices.reshape(4, 2, 4, 2, 2), ("y", "zh", "x", "core", "zl"))
    every = ("y", "zh", "x", "core", "zl")
    return jax.shard_map(
        on_device,
        mesh=inner,
        in_specs=(P("zl", SEQ, None, None), P("zl", SEQ, None, None), P("zl", None), P(), P(), P(), P(), P()),
        out_specs=(P("zl", SEQ, None, None), P(every, None), P(every, None), P(every), P(every)),
        check_vma=False,
    )
```

time: 280 us -> 238 us (0.85)
  Pallas kernels: 129 us -> 86.2 us
  waiting for transfers between devices: 92.2 us -> 69.3 us
  local copies, waits for them, and re-layouts: 5.67 us -> 25.5 us
  starting transfers between devices: 37.7 us -> 48.9 us
  other arithmetic: 14 us -> 5.88 us
    all_to_all x4, waiting for transfers between devices: 66.2 us -> 8.05 us  [the longest x2 6.75 us: to_owners(): lax.all_to_all(joined.reshape(count, rows // count, columns), axes, 0, 0,...]
    ppermute x2 -> x4, waiting for transfers between devices: 0.01 us -> 36.4 us  [the longest x2 28.3 us: halve(): lax.ppermute(held[half:], ('x', 'core'), neighbours(step))]
    unnamed x10 -> x52, local copies, waits for them, and re-layouts: 4.39 us -> 23 us
    pallas_call x1, Pallas kernels: 40.7 us -> 22.7 us  [forward(): pl.pallas_call(forward_kernel, grid=(SPAN,), in_specs=[full(rows.shape),...]
    pallas_call x4 -> x5, Pallas kernels: 74.9 us -> 58.3 us  [the longest x1 41.2 us: scores_backward(): pl.pallas_call(scores_kernel, grid_spec=pltpu.PrefetchScalarGridSpec(num_...]
    reshape x2 -> x0, other arithmetic: 8.64 us -> none  [reduce_rows(): joined.reshape(64, rows // 64, columns)]
    pallas_call x2 -> x1, Pallas kernels: 8.75 us -> 2.67 us  [split_patches(): pl.pallas_call(split_kernel, grid=(blocks // GROUP,), in_specs=[pl.BlockS...]
    ppermute x2 -> x4, starting transfers between devices: 0.19 us -> 5.82 us  [the longest x2 4.74 us: halve(): lax.ppermute(held[half:], ('x', 'core'), neighbours(step))]
  transfers between devices with their start and end apart: 7 -> 9, of which waited for: 4 -> 7; matrix products, arithmetic and copies ran while one was open for 5% -> 2% of each run, Pallas kernels for 37% -> 29%
where the time goes in v2:
time: 238 us; the launch traced here: 237 us
  Pallas kernels  86.2 us (36%)
  waiting for transfers between devices  69.3 us (29%)
  starting transfers between devices  48.9 us (21%)
  local copies, waits for them, and re-layouts  25.5 us (11%)
  other arithmetic  5.88 us (2%)
    pallas_call x1, Pallas kernels, scores_backward(): pl.pallas_call(scores_kernel, grid_spec=pltpu.PrefetchScalarGridSpec(num_...  41.2 us
    ppermute x2, waiting for transfers between devices, halve(): lax.ppermute(held[half:], ('x', 'core'), neighbours(step))  28.3 us
    all_to_all x1, waiting for transfers between devices, on_device(): rows_in = lax.all_to_all(split_patches(layer_input), SEQ, 0, 0, tiled=True)  24.9 us
    unnamed x52, local copies, waits for them, and re-layouts  23 us
    pallas_call x1, Pallas kernels, forward(): pl.pallas_call(forward_kernel, grid=(SPAN,), in_specs=[full(rows.shape),...  22.7 us
    all_to_all x2, starting transfers between devices, to_owners(): lax.all_to_all(joined.reshape(count, rows // count, columns), axes, 0, 0,...  16 us
    pallas_call x1, Pallas kernels, values_backward(): pl.pallas_call(values_kernel, grid_spec=pltpu.PrefetchScalarGridSpec(num_...  15.1 us
    all_to_all x1, starting transfers between devices, on_device(): rows_in = lax.all_to_all(split_patches(layer_input), SEQ, 0, 0, tiled=True)  11.7 us
  transfers between devices with their start and end apart: 9, of which 7 were waited for; matrix products, arithmetic and copies ran while one was open for 2% of the time, Pallas kernels for 29%

profile of v2, /device:TPU:0, one launch (start us, length us, event | category | flops | bytes accessed | tf_op | source)
XLA Modules:
  0.0 236.7 jit_solution(2144712979015789005)
XLA Ops:
  0.6 1.6 copy-done.6
  2.2 2.7 %split_patches.1 = bf16[64,16,1024]{2,1,0:T(8,128)(2,1)} custom-call(bf16[1,4,256,1024]{3,2,1,0:T(8,128)(2,1)S(1)} %copy-done.6), custom_call_target="tpu_custom_call" | custom-call | flops 536870912 | bytes 4194304 | tf_op jit(solution)/shard_map/split_patches/pallas_call | solution.py:89
  4.9 11.7 %all-to-all-start.1 = ((bf16[64,16,1024]{2,1,0:T(8,128)(2,1)}), bf16[64,16,1024]{2,1,0:T(8,128)(2,1)}, u32[]{:S(2)}, u32[]{:S(2)}) async-start(bf16[64,16,1024]{2,1,0:T(8,128)(2,1)} %split_patches.1), calls=%async_computation.1 | async-start | bytes 4194304 | tf_op jit(solution)/shard_map/all_to_all | solution.py:508
  16.6 0.3 reverse
  17.1 1.7 prepare.1
  18.8 1.3 copy-done.8
  20.1 2.0 copy-done.10
  22.1 24.9 %all-to-all-done.1.rows_ref = bf16[64,16,1024]{2,1,0:T(8,128)(2,1)} async-done(((bf16[64,16,1024]{2,1,0:T(8,128)(2,1)}), bf16[64,16,1024]{2,1,0:T(8,128)(2,1)}, u32[]{:S(2)}, u32[]{:S(2)}) %all-to-all-start.1) | async-done | bytes 2097184 | tf_op jit(solution)/shard_map/all_to_all | solution.py:508
  47.0 5.4 %all-to-all-start = ((bf16[64,16,1024]{2,1,0:T(8,128)(2,1)}), bf16[64,16,1024]{2,1,0:T(8,128)(2,1)S(1)}, u32[]{:S(2)}, u32[]{:S(2)}) async-start(bf16[64,16,1024]{2,1,0:T(8,128)(2,1)} %copy-done.8), calls=%async_computation | async-start | bytes 4194304 | tf_op jit(solution)/shard_map/all_to_all | solution.py:510
  52.4 2.2 copy-done.11
  54.6 22.7 %forward.1 = (bf16[4,256,1024]{2,1,0:T(8,128)(2,1)S(1)}, bf16[1024,1024]{1,0:T(8,128)(2,1)S(1)}, bf16[4,256,3072]{2,1,0:T(8,128)(2,1)}, bf16[4,16,256,256]{3,2,1,0:T(8,128)(2,1)}, bf16[4,256,1024]{2,1,0:T(8,128)(2,1)S(1)}) custom-call(bf16[64,16,1024]{2,1,0:T(8,128)(2,1)} %all-to-all-done.1.rows_ref, f32[1,1024]{1,0:T(1,128)S(1)} %bitcast.7, ...), custom_call_target="tpu_custom_call" | custom-call | flops 16000000000 | bytes 35651584 | tf_op jit(solution)/shard_map/forward/pallas_call | solution.py:222
  77.3 1.4 copy-done.16
  78.7 1.3 copy-done.20
  80.0 1.3 copy-done.22
  81.3 1.3 all-to-all-done.rows_ref
  82.6 1.6 copy-done.12
  84.2 1.6 copy-done.21
  85.8 15.1 %values_backward.1 = (bf16[4,256,1024]{2,1,0:T(8,128)(2,1)S(1)}, bf16[4,256,1024]{2,1,0:T(8,128)(2,1)S(1)}, bf16[4,256,1024]{2,1,0:T(8,128)(2,1)S(1)}, bf16[512,...) custom-call(s32[2,128]{1,0:T(2,128)S(1)} %pad_add_fusion.order_ref, bf16[64,16,1024]{2,1,0:T(8,128)(2,1)S(1)} %all-to-all-done.rows_ref, ...), custom_call_target="tpu_custom_call" | custom-call | flops 12000000000 | bytes 29360128 | tf_op jit(solution)/shard_map/values_backward/pallas_call | solution.py:307
  101.0 0.7 collective-permute-start
  101.7 3.8 %collective-permute-done = bf16[512,2048]{1,0:T(8,128)(2,1)S(1)} collective-permute-done((bf16[512,2048]{1,0:T(8,128)(2,1)S(1)}, bf16[512,2048]{1,0:T(8,128)(2,1)S(1)}, u32[]{:S(2)}, u32[]{:S(2)}) %collective-permute-start) | collective-permute-done | bytes 2097184 | tf_op jit(solution)/shard_map/ppermute | solution.py:497
  105.5 2.1 add_convert_fusion.1.joined_ref
  107.6 9.0 %all-to-all-start.2 = ((bf16[64,8,2048]{2,1,0:T(8,128)(2,1)}), bf16[64,8,2048]{2,1,0:T(8,128)(2,1)S(1)}, u32[]{:S(2)}, u32[]{:S(2)}) async-start(bf16[64,8,2048]{2,1,0:T(8,128)(2,1)} %bitcast.8), calls=%async_computation.2 | async-start | bytes 4194304 | tf_op jit(solution)/shard_map/all_to_all | solution.py:502
  116.6 41.2 %scores_backward.1 = (bf16[64,16,1024]{2,1,0:T(8,128)(2,1)}, bf16[512,2176]{1,0:T(8,128)(2,1)}, bf16[512,2176]{1,0:T(8,128)(2,1)}) custom-call(s32[2,128]{1,0:T(2,128)} %copy-done.9, bf16[512,2048]{1,0:T(8,128)(2,1)} %add_convert_fusion.1.joined_ref, bf16[4,16,256,256]{3,2,1,0:T(8,128)(2,1)} %get-tuple-element.26.weights_ref, ...), custom_call_target="tpu_custom_call" | custom-call | flops 24000000000 | bytes 35651584 | tf_op jit(solution)/shard_map/scores_backward/pallas_call | solution.py:400
  157.8 1.6 copy-done.2
  159.4 1.6 copy-done.3
  161.0 1.6 copy-done.5
  162.6 0.3 sum_parts.1
  163.0 0.3 collective-permute-start.1
  163.3 4.3 %collective-permute-done.1 = bf16[512,2176]{1,0:T(8,128)(2,1)S(1)} collective-permute-done((bf16[512,2176]{1,0:T(8,128)(2,1)S(1)}, bf16[512,2176]{1,0:T(8,128)(2,1)S(1)}, u32[]{:S(2)}, u32[]{:S(2)}) %collective-permute-start.1) | collective-permute-done | bytes 2228256 | tf_op jit(solution)/shard_map/ppermute | solution.py:497
  167.7 0.5 add_convert_fusion
  168.2 1.2 slice.40
  169.4 0.5 copy-done.23
  169.9 1.6 collective-permute-start.2
  171.5 10.0 %all-to-all-start.3 = ((bf16[64,16,1024]{2,1,0:T(8,128)(2,1)}), bf16[64,16,1024]{2,1,0:T(8,128)(2,1)S(1)}, u32[]{:S(2)}, u32[]{:S(2)}) async-start(bf16[64,16,1024]{2,1,0:T(8,128)(2,1)} %copy-done.4), calls=%async_computation.3 | async-start | bytes 4194304 | tf_op jit(solution)/shard_map/all_to_all | solution.py:523
  181.4 6.3 %collective-permute-done.2 = bf16[256,2176]{1,0:T(8,128)(2,1)S(1)} collective-permute-done((bf16[256,2176]{1,0:T(8,128)(2,1)}, bf16[256,2176]{1,0:T(8,128)(2,1)S(1)}, u32[]{:S(2)}, u32[]{:S(2)}) %collective-permute-start.2) | collective-permute-done | bytes 1114144 | tf_op jit(solution)/shard_map/ppermute | solution.py:493
  187.7 1.5 add_convert_fusion.2
  189.3 3.2 %collective-permute-start.3 = (bf16[128,2176]{1,0:T(8,128)(2,1)S(1)}, bf16[128,2176]{1,0:T(8,128)(2,1)S(1)}, u32[]{:S(2)}, u32[]{:S(2)}) collective-permute-start(bf16[128,2176]{1,0:T(8,128)(2,1)S(1)} %slice.42), channel_id=1, source_target_pairs={{0,12},{2,6},{4,8},{6,2},{8,4},{10,14},{12,0},{14,10},{1,13},{3,7}... | collective-permute-start | bytes 1671176 | tf_op jit(solution)/shard_map/ppermute | solution.py:493
  192.4 22.0 %collective-permute-done.3 = bf16[128,2176]{1,0:T(8,128)(2,1)S(1)} collective-permute-done((bf16[128,2176]{1,0:T(8,128)(2,1)S(1)}, bf16[128,2176]{1,0:T(8,128)(2,1)S(1)}, u32[]{:S(2)}, u32[]{:S(2)}) %collective-permute-start.3) | collective-permute-done | bytes 557088 | tf_op jit(solution)/shard_map/ppermute | solution.py:493
  214.4 1.0 add_convert_fusion.3.held_ref
  215.4 1.3 copy-done
  216.7 7.0 %all-to-all-start.4 = ((bf16[16,8,2176]{2,1,0:T(8,128)(2,1)}), bf16[16,8,2176]{2,1,0:T(8,128)(2,1)S(1)}, u32[]{:S(2)}, u32[]{:S(2)}) async-start(bf16[16,8,2176]{2,1,0:T(8,128)(2,1)} %bitcast.9), calls=%async_computation.4 | async-start | bytes 1114112 | tf_op jit(solution)/shard_map/all_to_all | solution.py:502
  223.8 0.6 fusion.8
  224.4 1.6 copy-done.1
  226.0 2.5 %merge_patches.1 = bf16[1,4,256,1024]{3,2,1,0:T(8,128)(2,1)} custom-call(bf16[64,16,1024]{2,1,0:T(8,128)(2,1)S(1)} %copy-done.1), custom_call_target="tpu_custom_call" | custom-call | flops 536870912 | bytes 4194304 | tf_op jit(solution)/shard_map/merge_patches/pallas_call | solution.py:108
  228.5 6.7 %all-to-all-done.4 = bf16[16,8,2176]{2,1,0:T(8,128)(2,1)S(1)} async-done(((bf16[16,8,2176]{2,1,0:T(8,128)(2,1)}), bf16[16,8,2176]{2,1,0:T(8,128)(2,1)S(1)}, u32[]{:S(2)}, u32[]{:S(2)}) %all-to-all-start.4) | async-done | bytes 557088 | tf_op jit(solution)/shard_map/all_to_all | solution.py:502
  235.2 0.1 convert_reduce_fusion
  235.3 0.7 slice_reduce_fusion
  236.0 0.6 pad_maximum_fusion
  (47 shorter events, 0.3 us)
Async XLA Ops:
  0.6 1.6 copy-start.6
  4.9 11.7 %copy-start.24 = (f32[16,511]{1,0:T(8,128)S(1)}, f32[16,511]{1,0:T(8,128)}, u32[]{:S(2)}) copy-start(f32[16,511]{1,0:T(8,128)} %param.15) | copy-start | bytes 98116
  4.9 12.2 %copy-start.7 = (bf16[1,4,256,1024]{3,2,1,0:T(8,128)(2,1)S(1)}, bf16[1,4,256,1024]{3,2,1,0:T(8,128)(2,1)}, u32[]{:S(2)}) copy-start(bf16[1,4,256,1024]{3,2,1,0:T(8,128)(2,1)} %rows_ref.2) | copy-start | bytes 6291460
  4.9 42.1 %all-to-all-start.1 = ((bf16[64,16,1024]{2,1,0:T(8,128)(2,1)}), bf16[64,16,1024]{2,1,0:T(8,128)(2,1)}, u32[]{:S(2)}, u32[]{:S(2)}) async-start(bf16[64,16,1024]{2,1,0:T(8,128)(2,1)} %split_patches.1), calls=%async_computation.1 | async-start | bytes 4194304 | tf_op jit(solution)/shard_map/all_to_all | solution.py:508
  18.8 1.3 copy-start.8
  20.1 2.0 copy-start.10
  47.0 5.4 %copy-start.13 = (f32[1024]{0:T(1024)S(1)}, f32[1024]{0:T(1024)}, u32[]{:S(2)}) copy-start(f32[1024]{0:T(1024)} %param.12) | copy-start | bytes 12292
  47.0 5.4 %copy-start.14 = (f32[1024]{0:T(1024)S(1)}, f32[1024]{0:T(1024)}, u32[]{:S(2)}) copy-start(f32[1024]{0:T(1024)} %param.11) | copy-start | bytes 12292
  47.0 35.7 %all-to-all-start = ((bf16[64,16,1024]{2,1,0:T(8,128)(2,1)}), bf16[64,16,1024]{2,1,0:T(8,128)(2,1)S(1)}, u32[]{:S(2)}, u32[]{:S(2)}) async-start(bf16[64,16,1024]{2,1,0:T(8,128)(2,1)} %copy-done.8), calls=%async_computation | async-start | bytes 4194304 | tf_op jit(solution)/shard_map/all_to_all | solution.py:510
  52.4 30.3 %copy-start.9 = (s32[2,128]{1,0:T(2,128)}, s32[2,128]{1,0:T(2,128)S(1)}, u32[]{:S(2)}) copy-start(s32[2,128]{1,0:T(2,128)S(1)} %pad_add_fusion.order_ref) | copy-start | bytes 3076
  52.4 2.2 copy-start.11
  54.6 28.0 %copy-start.15 = (s32[1,256]{1,0:T(1,128)S(1)}, s32[1,256]{1,0:T(1,128)}, u32[]{:S(2)}) copy-start(s32[1,256]{1,0:T(1,128)} %slot_ref.1) | copy-start | bytes 3076
  77.3 1.4 copy-start.16
  78.7 1.3 copy-start.20
  80.0 1.4 copy-start.22
  82.6 1.6 copy-start.12
  84.2 1.6 copy-start.21
  101.0 6.7 %copy-start.17 = (bf16[4,256,1024]{2,1,0:T(8,128)(2,1)}, bf16[4,256,1024]{2,1,0:T(8,128)(2,1)S(1)}, u32[]{:S(2)}) copy-start(bf16[4,256,1024]{2,1,0:T(8,128)(2,1)S(1)} %get-tuple-element.34.grad_ref) | copy-start | bytes 6291460
  101.0 6.6 %copy-start.18 = (bf16[4,256,1024]{2,1,0:T(8,128)(2,1)}, bf16[4,256,1024]{2,1,0:T(8,128)(2,1)S(1)}, u32[]{:S(2)}) copy-start(bf16[4,256,1024]{2,1,0:T(8,128)(2,1)S(1)} %get-tuple-element.32.att_grad_ref) | copy-start | bytes 6291460
  101.0 6.6 %copy-start.19 = (bf16[4,256,1024]{2,1,0:T(8,128)(2,1)}, bf16[4,256,1024]{2,1,0:T(8,128)(2,1)S(1)}, u32[]{:S(2)}) copy-start(bf16[4,256,1024]{2,1,0:T(8,128)(2,1)S(1)} %get-tuple-element.33.val_grad_ref) | copy-start | bytes 6291460
  101.0 4.5 %collective-permute-start = (bf16[512,2048]{1,0:T(8,128)(2,1)S(1)}, bf16[512,2048]{1,0:T(8,128)(2,1)S(1)}, u32[]{:S(2)}, u32[]{:S(2)}) collective-permute-start(bf16[512,2048]{1,0:T(8,128)(2,1)S(1)} %get-tuple-element.30), channel_id=1, source_target_pairs={{0,2},{2,0},{1,3},{3,1},{4,6},{6,4},{5,7},{7,5},{8,10},{10,8},{9,1... | collective-permute-start | bytes 6291464 | tf_op jit(solution)/shard_map/ppermute | solution.py:497
  107.6 50.2 %all-to-all-start.2 = ((bf16[64,8,2048]{2,1,0:T(8,128)(2,1)}), bf16[64,8,2048]{2,1,0:T(8,128)(2,1)S(1)}, u32[]{:S(2)}, u32[]{:S(2)}) async-start(bf16[64,8,2048]{2,1,0:T(8,128)(2,1)} %bitcast.8), calls=%async_computation.2 | async-start | bytes 4194304 | tf_op jit(solution)/shard_map/all_to_all | solution.py:502
  157.8 1.6 copy-start.2
  159.4 1.6 copy-start.3
  161.0 1.6 copy-start.5
  163.0 5.2 %copy-start.4 = (bf16[64,16,1024]{2,1,0:T(8,128)(2,1)}, bf16[64,16,1024]{2,1,0:T(8,128)(2,1)S(1)}, u32[]{:S(2)}) copy-start(bf16[64,16,1024]{2,1,0:T(8,128)(2,1)S(1)} %get-tuple-element.39) | copy-start | bytes 6291460
  163.0 4.7 %collective-permute-start.1 = (bf16[512,2176]{1,0:T(8,128)(2,1)S(1)}, bf16[512,2176]{1,0:T(8,128)(2,1)S(1)}, u32[]{:S(2)}, u32[]{:S(2)}) collective-permute-start(bf16[512,2176]{1,0:T(8,128)(2,1)S(1)} %get-tuple-element.41), channel_id=1, source_target_pairs={{0,2},{2,0},{1,3},{3,1},{4,6},{6,4},{5,7},{7,5},{8,10},{10,8},{9,1... | collective-permute-start | bytes 6684680 | tf_op jit(solution)/shard_map/ppermute | solution.py:497
  168.2 1.7 copy-start.23
  169.9 17.8 %collective-permute-start.2 = (bf16[256,2176]{1,0:T(8,128)(2,1)}, bf16[256,2176]{1,0:T(8,128)(2,1)S(1)}, u32[]{:S(2)}, u32[]{:S(2)}) collective-permute-start(bf16[256,2176]{1,0:T(8,128)(2,1)} %slice.40), channel_id=1, source_target_pairs={{0,4},{2,14},{4,0},{6,10},{8,12},{10,6},{12,8},{14,2},{1,5},{3,15}... | collective-permute-start | bytes 3342344 | tf_op jit(solution)/shard_map/ppermute | solution.py:493
  171.5 43.9 %all-to-all-start.3 = ((bf16[64,16,1024]{2,1,0:T(8,128)(2,1)}), bf16[64,16,1024]{2,1,0:T(8,128)(2,1)S(1)}, u32[]{:S(2)}, u32[]{:S(2)}) async-start(bf16[64,16,1024]{2,1,0:T(8,128)(2,1)} %copy-done.4), calls=%async_computation.3 | async-start | bytes 4194304 | tf_op jit(solution)/shard_map/all_to_all | solution.py:523
  189.3 25.2 %collective-permute-start.3 = (bf16[128,2176]{1,0:T(8,128)(2,1)S(1)}, bf16[128,2176]{1,0:T(8,128)(2,1)S(1)}, u32[]{:S(2)}, u32[]{:S(2)}) collective-permute-start(bf16[128,2176]{1,0:T(8,128)(2,1)S(1)} %slice.42), channel_id=1, source_target_pairs={{0,12},{2,6},{4,8},{6,2},{8,4},{10,14},{12,0},{14,10},{1,13},{3,7}... | collective-permute-start | bytes 1671176 | tf_op jit(solution)/shard_map/ppermute | solution.py:493
  215.4 1.3 copy-start
  216.7 18.5 %all-to-all-start.4 = ((bf16[16,8,2176]{2,1,0:T(8,128)(2,1)}), bf16[16,8,2176]{2,1,0:T(8,128)(2,1)S(1)}, u32[]{:S(2)}, u32[]{:S(2)}) async-start(bf16[16,8,2176]{2,1,0:T(8,128)(2,1)} %bitcast.9), calls=%async_computation.4 | async-start | bytes 1114112 | tf_op jit(solution)/shard_map/all_to_all | solution.py:502
  224.4 1.6 copy-start.1

commit v3 on v2

--- a/solution.py
+++ b/solution.py
@@ -176,7 +176,7 @@
 
 def forward_kernel(
     rows_ref, gain_ref, bias_ref, w_ref, table_ref,
-    places_ref, turned_ref, proj_ref, weights_ref, att_ref, places,
+    places_ref, turned_ref, proj_ref, weights_ref, natural_ref, att_ref, places,
 ):
     step = pl.program_id(0)
 
@@ -210,7 +210,9 @@
             total = jnp.sum(raised, axis=0, keepdims=True)
             short = (raised * (1.0 / total)).astype(BF)
             weights_ref[0, 2 * i + h] = short
-            parts.append(mm(short, vals, TN))
+            natural = short.T
+            natural_ref[0, 2 * i + h] = natural
+            parts.append(mm(natural, vals))
         att_ref[0, :, lanes] = jnp.where(first, parts[0], parts[1]).astype(BF)
 
 
@@ -229,12 +231,14 @@
             pl.BlockSpec((width, frames), lambda p: (0, p)),
             per(frames, 3 * width),
             per(heads, frames, frames),
+            per(heads, frames, frames),
             per(frames, width),
         ],
         out_shape=[
             jax.ShapeDtypeStruct((SPAN, frames, width), BF),
             jax.ShapeDtypeStruct((width, SPAN * frames), BF),
             jax.ShapeDtypeStruct((SPAN, frames, 3 * width), BF),
+            jax.ShapeDtypeStruct((SPAN, heads, frames, frames), BF),
             jax.ShapeDtypeStruct((SPAN, heads, frames, frames), BF),
             jax.ShapeDtypeStruct((SPAN, frames, width), BF),
         ],
@@ -327,10 +331,20 @@
 
 
 def scores_kernel(
-    order_ref, joined_ref, weights_ref, proj_ref, att_grad_ref, val_grad_ref, grad_ref, places_ref, w_ref, gain_ref,
-    turned_ref, out_ref, keep_ref, send_ref, results, pairs, sums, terms,
+    order_ref, joined_ref, weights_ref, natural_ref, proj_ref, att_grad_ref, val_grad_ref, grad_ref, places_ref, w_far, gain_ref,
+    turned_far, out_ref, keep_ref, send_ref, results, pairs, sums, terms, w_ref, turned_ref, arrived,
 ):
     step = pl.program_id(0)
+    copies = [
+        pltpu.make_async_copy(w_far, w_ref, arrived.at[0]),
+        pltpu.make_async_copy(turned_far, turned_ref, arrived.at[1]),
+    ]
+
+    @pl.when(step == 0)
+    def _():
+        for copy in copies:
+            copy.start()
+
     frames, width = grad_ref.shape[1:]
     first = halves(frames)
     factor = 0.125
@@ -350,9 +364,17 @@
             shared = jnp.sum(weight_grad * weights, axis=0, keepdims=True)
             score_grad = (weights * (weight_grad - shared)).astype(BF)
             key_parts.append(mm(score_grad, queries))
-            query_parts.append(mm(score_grad, keys, TN))
+            weight_grad = mm(jnp.where(first if h == 0 else ~first, att_grad, jnp.zeros_like(att_grad)), vals, NT)
+            weights = natural_ref[0, 2 * i + h].astype(F32)
+            shared = jnp.sum(weight_grad * weights, axis=1, keepdims=True)
+            query_parts.append(mm((weights * (weight_grad - shared)).astype(BF), keys))
         pairs[here, lanes] = (jnp.where(first, query_parts[0], query_parts[1]) * factor).astype(BF)
         pairs[here, key_lanes] = jnp.where(first, key_parts[0], key_parts[1]).astype(BF)
+
+    @pl.when(step == 0)
+    def _():
+        for copy in copies:
+            copy.wait()
 
     hidden_grad = mm(pairs[here, :], w_ref[:, : 2 * width], NT) + mm(val_grad_ref[0], w_ref[:, 2 * width :], NT)
     normed, inv_std = norm_parts(places_ref[0].astype(F32))
@@ -389,7 +411,7 @@
         place_rows(terms.at[:, :PAIR], order_ref, 1, keep_ref, send_ref, slice(2 * width, 2 * width + PAIR))
 
 
-def scores_backward(order, joined, weights, proj, att_grad, val_grad, grads, places, w_qkv, gain, turned):
+def scores_backward(order, joined, weights, natural, proj, att_grad, val_grad, grads, places, w_qkv, gain, turned):
     _, frames, width = grads.shape
     heads = weights.shape[1]
     blocks = frames // SPAN
@@ -402,43 +424,26 @@
         grid_spec=pltpu.PrefetchScalarGridSpec(
             num_scalar_prefetch=1,
             grid=(SPAN,),
-            in_specs=[pl.BlockSpec(memory_space=pl.ANY), per(heads, frames, frames), per(frames, 3 * width),
+            in_specs=[pl.BlockSpec(memory_space=pl.ANY), per(heads, frames, frames), per(heads, frames, frames),
+                      per(frames, 3 * width),
                       per(frames, width), per(frames, width), per(frames, width), per(frames, width),
-                      full(w_qkv.shape), full((1, width)), full(turned.shape)],
+                      pl.BlockSpec(memory_space=pl.ANY), full((1, width)), pl.BlockSpec(memory_space=pl.ANY)],
             out_specs=[full(o.shape) for o in outs],
             scratch_shapes=[
                 pltpu.VMEM((SPAN, frames, width), BF),
                 pltpu.VMEM((tokens, 2 * width), BF),
                 pltpu.VMEM((8, width), F32),
                 pltpu.VMEM((width, 256), F32),
+                pltpu.VMEM(w_qkv.shape, BF),
+                pltpu.VMEM(turned.shape, BF),
+                pltpu.SemaphoreType.DMA((2,)),
             ],
         ),
         out_shape=outs,
         compiler_params=pltpu.CompilerParams(vmem_limit_bytes=SCORES_VMEM),
         cost_estimate=cost(24 * 10**9, 34 * 2**20),
         name="scores_backward",
-    )(order, joined, weights, proj, att_grad, val_grad, grads, places, w_qkv, gain, turned)
-
-
-def total_kernel(parts_ref, *refs):
-    total_ref = refs[len(refs) // 2]
-    total_ref[...] = jnp.sum(parts_ref[...].astype(F32), axis=0)
-
-
-def sum_parts(parts, *passed):
-    anywhere = [pl.BlockSpec(memory_space=pltpu.HBM)] * len(passed)
-    here = pl.BlockSpec(memory_space=pltpu.VMEM)
-    return pl.pallas_call(
-        total_kernel,
-        in_specs=[here] + anywhere,
-        out_specs=[here] + anywhere,
-        out_shape=[jax.ShapeDtypeStruct(parts.shape[1:], F32)]
-        + [jax.ShapeDtypeStruct(p.shape, p.dtype) for p in passed],
-        input_output_aliases={i + 1: i + 1 for i in range(len(passed))},
-        compiler_params=params(),
-        cost_estimate=cost(parts.size, 2 * parts.size),
-        name="sum_parts",
-    )(parts, *passed)
+    )(order, joined, weights, natural, proj, att_grad, val_grad, grads, places, w_qkv, gain, turned)
 
 
 def gray(place):
@@ -468,29 +473,36 @@
     return pairs
 
 
-def after_kernel(held_ref, other_ref, out_ref):
-    del held_ref, other_ref, out_ref
-
-
-def after(held, other):
-    anywhere = pl.BlockSpec(memory_space=pltpu.HBM)
+def after_kernel(*refs):
+    del refs
+
+
+def after(other, *held, space=pltpu.HBM, room=SCORES_VMEM):
+    anywhere = pl.BlockSpec(memory_space=space)
     return pl.pallas_call(
         after_kernel,
-        in_specs=[anywhere, anywhere],
-        out_specs=anywhere,
-        out_shape=jax.ShapeDtypeStruct(held.shape, held.dtype),
-        input_output_aliases={0: 0},
+        in_specs=[anywhere] * (len(held) + 1),
+        out_specs=[anywhere] * len(held),
+        out_shape=[jax.ShapeDtypeStruct(h.shape, h.dtype) for h in held],
+        input_output_aliases={i + 1: i for i in range(len(held))},
+        compiler_params=pltpu.CompilerParams(vmem_limit_bytes=room),
         name="after",
-    )(held, other)
+    )(other, *held)
 
 
 def add(a, b):
     return (a.astype(F32) + b.astype(F32)).astype(BF)
 
 
-def halve(held, step):
+def halves_sum(held, got):
     half = held.shape[0] // 2
-    return add(held[:half], lax.ppermute(held[half:], ("x", "core"), neighbours(step)))
+    return add(held[:half], got[:half]), add(held[half:], got[half:])
+
+
+def sum_along_x(keep, send):
+    keep, send = halves_sum(keep, lax.ppermute(send, "core", [(0, 1), (1, 0)]))
+    keep, send = halves_sum(keep, lax.ppermute(send, ("x", "core"), neighbours(0)))
+    return add(keep, lax.ppermute(send, ("x", "core"), neighbours(1)))
 
 
 def join_cores(keep, send):
@@ -510,20 +522,21 @@
     rows_grad = lax.all_to_all(split_grad, SEQ, 0, 0, tiled=True)
     orders = row_orders()
     gain, bias = ln_gain.reshape(1, width), ln_bias.reshape(1, width)
-    places, turned, proj, weights, att = forward(rows_in, gain, bias, w_qkv, table)
+    places, turned, proj, weights, natural, att = forward(rows_in, gain, bias, w_qkv, table)
     grads, att_grad, val_grad, keep, send = values_backward(
         orders, rows_grad, slot_frame, w_out, weights, att, turned
     )
     joined = join_cores(keep, send)
     parts = to_owners(joined, CHIPS, 64)
     out_rows, keep, send = scores_backward(
-        orders, joined, weights, proj, att_grad, val_grad, grads, places, w_qkv, gain, turned
+        orders, joined, weights, natural, proj, att_grad, val_grad, grads, places, w_qkv, gain, turned
     )
-    first_sums, out_rows, keep, send = sum_parts(parts, out_rows, keep, send)
+    out_rows, keep, send = after(parts, out_rows, keep, send)
     out_parts = lax.all_to_all(out_rows, SEQ, 0, 0, tiled=True)
-    held = halve(halve(join_cores(keep, send), 0), 1)
+    held = sum_along_x(keep, send)
     in_grad = merge_patches(out_parts)
-    held = after(held, out_parts)
+    (held,) = after(out_parts, held, space=pl.ANY, room=2**20)
+    first_sums = jnp.sum(parts.astype(F32), axis=0)
     second_sums = jnp.sum(to_owners(held, PLANE, 16).astype(F32), axis=0)
     tokens = 128 * SPAN * frames
     scale = float(tokens) ** (-0.5)

time: 238 us -> 232 us (0.975)
  local copies, waits for them, and re-layouts: 25.5 us -> 17.3 us
  other arithmetic: 5.88 us -> 11.2 us
  Pallas kernels: 86.2 us -> 83.1 us
    unnamed x52 -> x40, local copies, waits for them, and re-layouts: 23 us -> 16 us
    ppermute x2 -> x1, waiting for transfers between devices: 8.12 us -> 3.79 us  [join_cores(): return add(keep, lax.ppermute(send, 'core', [(0, 1), (1, 0)]))]
    pallas_call x1, Pallas kernels: 41.2 us -> 37.2 us  [scores_backward(): pl.pallas_call(scores_kernel, grid_spec=pltpu.PrefetchScalarGridSpec(num_...]
    convert_element_type x4, other arithmetic: 5.09 us -> 8.54 us  [add(): return (a.astype(F32) + b.astype(F32)).astype(BF)]
    ppermute x2 -> x3, waiting for transfers between devices: 28.3 us -> 31.2 us  [the longest x1 20.4 us: sum_along_x(): return add(keep, lax.ppermute(send, ('x', 'core'), neighbours(1)))]
    ppermute x2 -> x3, starting transfers between devices: 4.74 us -> 4.84 us  [the longest x1 3.26 us: sum_along_x(): return add(keep, lax.ppermute(send, ('x', 'core'), neighbours(1)))]
  transfers between devices with their start and end apart: 9 -> 9, of which waited for: 7 -> 7; matrix products, arithmetic and copies ran while one was open for 2% -> 3% of each run, Pallas kernels for 29% -> 28%
where the time goes in v3:
time: 232 us; the launch traced here: 231 us
  Pallas kernels  83.1 us (36%)
  waiting for transfers between devices  68.4 us (29%)
  starting transfers between devices  49.8 us (21%)
  local copies, waits for them, and re-layouts  17.3 us (7%)
  other arithmetic  11.2 us (5%)
    pallas_call x1, Pallas kernels, scores_backward(): pl.pallas_call(scores_kernel, grid_spec=pltpu.PrefetchScalarGridSpec(num_...  37.2 us
    all_to_all x1, waiting for transfers between devices, on_device(): rows_in = lax.all_to_all(split_patches(layer_input), SEQ, 0, 0, tiled=True)  24.9 us
    pallas_call x1, Pallas kernels, forward(): pl.pallas_call(forward_kernel, grid=(SPAN,), in_specs=[full(rows.shape),...  23.9 us
    ppermute x1, waiting for transfers between devices, sum_along_x(): return add(keep, lax.ppermute(send, ('x', 'core'), neighbours(1)))  20.4 us
    all_to_all x2, starting transfers between devices, to_owners(): lax.all_to_all(joined.reshape(count, rows // count, columns), axes, 0, 0,...  17.2 us
    unnamed x40, local copies, waits for them, and re-layouts  16 us
    pallas_call x1, Pallas kernels, values_backward(): pl.pallas_call(values_kernel, grid_spec=pltpu.PrefetchScalarGridSpec(num_...  15.1 us
    all_to_all x1, starting transfers between devices, on_device(): rows_in = lax.all_to_all(split_patches(layer_input), SEQ, 0, 0, tiled=True)  11.7 us
  transfers between devices with their start and end apart: 9, of which 7 were waited for; matrix products, arithmetic and copies ran while one was open for 3% of the time, Pallas kernels for 28%

profile of v3, /device:TPU:0, one launch (start us, length us, event | category | flops | bytes accessed | tf_op | source)
XLA Modules:
  0.0 230.7 jit_solution(15278957190328391587)
XLA Ops:
  0.6 1.6 copy-done
  2.2 2.7 %split_patches.1 = bf16[64,16,1024]{2,1,0:T(8,128)(2,1)} custom-call(bf16[1,4,256,1024]{3,2,1,0:T(8,128)(2,1)S(1)} %copy-done), custom_call_target="tpu_custom_call" | custom-call | flops 536870912 | bytes 4194304 | tf_op jit(solution)/shard_map/split_patches/pallas_call | solution.py:89
  4.9 11.7 %all-to-all-start.1 = ((bf16[64,16,1024]{2,1,0:T(8,128)(2,1)}), bf16[64,16,1024]{2,1,0:T(8,128)(2,1)}, u32[]{:S(2)}, u32[]{:S(2)}) async-start(bf16[64,16,1024]{2,1,0:T(8,128)(2,1)} %split_patches.1), calls=%async_computation.1 | async-start | bytes 4194304 | tf_op jit(solution)/shard_map/all_to_all | solution.py:520
  16.7 0.3 reverse
  17.0 0.1 slice.76
  17.1 1.7 prepare.1
  18.8 0.0 copy-start.2
  18.8 1.3 copy-done.2
  20.1 2.0 copy-done.4
  22.0 24.9 %all-to-all-done.1.rows_ref = bf16[64,16,1024]{2,1,0:T(8,128)(2,1)} async-done(((bf16[64,16,1024]{2,1,0:T(8,128)(2,1)}), bf16[64,16,1024]{2,1,0:T(8,128)(2,1)}, u32[]{:S(2)}, u32[]{:S(2)}) %all-to-all-start.1) | async-done | bytes 2097184 | tf_op jit(solution)/shard_map/all_to_all | solution.py:520
  47.0 5.4 %all-to-all-start = ((bf16[64,16,1024]{2,1,0:T(8,128)(2,1)}), bf16[64,16,1024]{2,1,0:T(8,128)(2,1)S(1)}, u32[]{:S(2)}, u32[]{:S(2)}) async-start(bf16[64,16,1024]{2,1,0:T(8,128)(2,1)} %copy-done.2), calls=%async_computation | async-start | bytes 4194304 | tf_op jit(solution)/shard_map/all_to_all | solution.py:522
  52.4 0.0 copy-start.3
  52.4 2.2 copy-done.5
  54.6 23.9 %forward.1 = (bf16[4,256,1024]{2,1,0:T(8,128)(2,1)S(1)}, bf16[1024,1024]{1,0:T(8,128)(2,1)S(1)}, bf16[4,256,3072]{2,1,0:T(8,128)(2,1)}, bf16[4,16,256,256]{3,2,1...) custom-call(bf16[64,16,1024]{2,1,0:T(8,128)(2,1)} %all-to-all-done.1.rows_ref, ...), custom_call_target="tpu_custom_call" | custom-call | flops 16000000000 | bytes 35651584 | tf_op jit(solution)/shard_map/forward/pallas_call | solution.py:224
  78.5 1.3 copy-done.10
  79.8 1.4 copy-done.14
  81.2 1.3 copy-done.16
  82.5 0.1 all-to-all-done.rows_ref
  82.7 1.6 copy-done.6
  84.3 1.6 copy-done.15
  85.8 15.1 %values_backward.1 = (bf16[4,256,1024]{2,1,0:T(8,128)(2,1)S(1)}, bf16[4,256,1024]{2,1,0:T(8,128)(2,1)S(1)}, bf16[4,256,1024]{2,1,0:T(8,128)(2,1)S(1)}, bf16[512,...) custom-call(s32[2,128]{1,0:T(2,128)S(1)} %pad_add_fusion.order_ref, bf16[64,16,1024]{2,1,0:T(8,128)(2,1)S(1)} %all-to-all-done.rows_ref, ...), custom_call_target="tpu_custom_call" | custom-call | flops 12000000000 | bytes 29360128 | tf_op jit(solution)/shard_map/values_backward/pallas_call | solution.py:311
  101.0 0.7 collective-permute-start
  101.7 3.8 %collective-permute-done = bf16[512,2048]{1,0:T(8,128)(2,1)S(1)} collective-permute-done((bf16[512,2048]{1,0:T(8,128)(2,1)S(1)}, bf16[512,2048]{1,0:T(8,128)(2,1)S(1)}, u32[]{:S(2)}, u32[]{:S(2)}) %collective-permute-start) | collective-permute-done | bytes 2097184 | tf_op jit(solution)/shard_map/ppermute | solution.py:509
  105.5 2.1 add_convert_fusion.joined_ref
  107.6 10.2 %all-to-all-start.2 = ((bf16[64,8,2048]{2,1,0:T(8,128)(2,1)}), bf16[64,8,2048]{2,1,0:T(8,128)(2,1)S(1)}, u32[]{:S(2)}, u32[]{:S(2)}) async-start(bf16[64,8,2048]{2,1,0:T(8,128)(2,1)} %bitcast.8), calls=%async_computation.2 | async-start | bytes 4194304 | tf_op jit(solution)/shard_map/all_to_all | solution.py:514
  117.8 37.2 %scores_backward.1 = (bf16[64,16,1024]{2,1,0:T(8,128)(2,1)}, bf16[512,2176]{1,0:T(8,128)(2,1)}, bf16[512,2176]{1,0:T(8,128)(2,1)}) custom-call(s32[2,128]{1,0:T(2,128)} %copy-done.3, bf16[512,2048]{1,0:T(8,128)(2,1)} %add_convert_fusion.joined_ref, bf16[4,16,256,256]{3,2,1,0:T(8,128)(2,1)} %get-tuple-element.26.weights_ref, ...), custom_call_target="tpu_custom_call" | custom-call | flops 24000000000 | bytes 35651584 | tf_op jit(solution)/shard_map/scores_backward/pallas_call | solution.py:422
  155.0 0.0 all-to-all-done.2.refs_0_
  155.1 0.0 copy-start.17
  155.1 1.3 copy-done.17
  156.4 0.0 collective-permute-start.1
  156.4 4.6 %collective-permute-done.1 = bf16[512,2176]{1,0:T(8,128)(2,1)S(1)} collective-permute-done((bf16[512,2176]{1,0:T(8,128)(2,1)}, bf16[512,2176]{1,0:T(8,128)(2,1)S(1)}, u32[]{:S(2)}, u32[]{:S(2)}) %collective-permute-start.1) | collective-permute-done | bytes 2228256 | tf_op jit(solution)/shard_map/ppermute | solution.py:503
  160.9 3.2 %add_convert_fusion.2 = (bf16[256,2176]{1,0:T(8,128)(2,1)S(1)}, bf16[256,2176]{1,0:T(8,128)(2,1)}) fusion(bf16[512,2176]{1,0:T(8,128)(2,1)S(1)} %collective-permute-done.1, bf16[512,2176]{1,0:T(8,128)(2,1)} %get-tuple-element.41), kind=kLoop, calls=%fused_computation.3 | loop fusion | flops 4456448 | bytes 6684672 | tf_op jit(solution)/shard_map/convert_element_type | solution.py:494
  164.1 1.6 collective-permute-start.2
  165.7 10.0 %all-to-all-start.3 = ((bf16[64,16,1024]{2,1,0:T(8,128)(2,1)}), bf16[64,16,1024]{2,1,0:T(8,128)(2,1)S(1)}, u32[]{:S(2)}, u32[]{:S(2)}) async-start(bf16[64,16,1024]{2,1,0:T(8,128)(2,1)} %get-tuple-element.40), calls=%async_computation.3 | async-start | bytes 4194304 | tf_op jit(solution)/shard_map/all_to_all | solution.py:535
  175.7 6.3 %collective-permute-done.2 = bf16[256,2176]{1,0:T(8,128)(2,1)} collective-permute-done((bf16[256,2176]{1,0:T(8,128)(2,1)}, bf16[256,2176]{1,0:T(8,128)(2,1)}, u32[]{:S(2)}, u32[]{:S(2)}) %collective-permute-start.2) | collective-permute-done | bytes 1114144 | tf_op jit(solution)/shard_map/ppermute | solution.py:504
  181.9 1.2 add_convert_fusion.4
  183.1 3.3 %collective-permute-start.3 = (bf16[128,2176]{1,0:T(8,128)(2,1)S(1)}, bf16[128,2176]{1,0:T(8,128)(2,1)S(1)}, u32[]{:S(2)}, u32[]{:S(2)}) collective-permute-start(bf16[128,2176]{1,0:T(8,128)(2,1)S(1)} %add_convert_fusion.4), channel_id=1, source_target_pairs={{0,12},{2,6},{4,8},{6,2},{8,4},{10,14},{12,0},{14,10},{1,13},{3,7}... | collective-permute-start | bytes 1671176 | tf_op jit(solution)/shard_map/ppermute | solution.py:505
  186.4 1.9 convert_reduce_fusion
  188.3 20.4 %collective-permute-done.3 = bf16[128,2176]{1,0:T(8,128)(2,1)S(1)} collective-permute-done((bf16[128,2176]{1,0:T(8,128)(2,1)S(1)}, bf16[128,2176]{1,0:T(8,128)(2,1)S(1)}, u32[]{:S(2)}, u32[]{:S(2)}) %collective-permute-start.3) | collective-permute-done | bytes 557088 | tf_op jit(solution)/shard_map/ppermute | solution.py:505
  208.6 2.1 add_convert_fusion.3.refs_1_
  210.7 0.0 all-to-all-done.3.rows_ref.refs_0_
  210.7 7.0 %all-to-all-start.4 = ((bf16[16,8,2176]{2,1,0:T(8,128)(2,1)}), bf16[16,8,2176]{2,1,0:T(8,128)(2,1)S(1)}, u32[]{:S(2)}, u32[]{:S(2)}) async-start(bf16[16,8,2176]{2,1,0:T(8,128)(2,1)} %bitcast.3), calls=%async_computation.4 | async-start | bytes 1114112 | tf_op jit(solution)/shard_map/all_to_all | solution.py:514
  217.8 0.6 fusion.8
  218.4 2.5 %merge_patches.1 = bf16[1,4,256,1024]{3,2,1,0:T(8,128)(2,1)} custom-call(bf16[64,16,1024]{2,1,0:T(8,128)(2,1)S(1)} %all-to-all-done.3.rows_ref.refs_0_), custom_call_target="tpu_custom_call" | custom-call | flops 536870912 | bytes 4194304 | tf_op jit(solution)/shard_map/merge_patches/pallas_call | solution.py:108
  220.9 8.3 %all-to-all-done.4 = bf16[16,8,2176]{2,1,0:T(8,128)(2,1)S(1)} async-done(((bf16[16,8,2176]{2,1,0:T(8,128)(2,1)}), bf16[16,8,2176]{2,1,0:T(8,128)(2,1)S(1)}, u32[]{:S(2)}, u32[]{:S(2)}) %all-to-all-start.4) | async-done | bytes 557088 | tf_op jit(solution)/shard_map/all_to_all | solution.py:514
  229.2 0.1 convert_reduce_fusion.1
  229.3 0.7 slice_reduce_fusion
  230.0 0.6 pad_maximum_fusion
  (34 shorter events, 0.1 us)
Async XLA Ops:
  0.6 1.6 copy-start
  4.9 11.7 %copy-start.18 = (f32[16,511]{1,0:T(8,128)S(1)}, f32[16,511]{1,0:T(8,128)}, u32[]{:S(2)}) copy-start(f32[16,511]{1,0:T(8,128)} %param.15) | copy-start | bytes 98116
  4.9 12.2 %copy-start.1 = (bf16[1,4,256,1024]{3,2,1,0:T(8,128)(2,1)S(1)}, bf16[1,4,256,1024]{3,2,1,0:T(8,128)(2,1)}, u32[]{:S(2)}) copy-start(bf16[1,4,256,1024]{3,2,1,0:T(8,128)(2,1)} %rows_ref.2) | copy-start | bytes 6291460
  4.9 42.1 %all-to-all-start.1 = ((bf16[64,16,1024]{2,1,0:T(8,128)(2,1)}), bf16[64,16,1024]{2,1,0:T(8,128)(2,1)}, u32[]{:S(2)}, u32[]{:S(2)}) async-start(bf16[64,16,1024]{2,1,0:T(8,128)(2,1)} %split_patches.1), calls=%async_computation.1 | async-start | bytes 4194304 | tf_op jit(solution)/shard_map/all_to_all | solution.py:520
  18.8 1.3 copy-start.2
  20.1 2.0 copy-start.4
  47.0 5.4 %copy-start.7 = (f32[1024]{0:T(1024)S(1)}, f32[1024]{0:T(1024)}, u32[]{:S(2)}) copy-start(f32[1024]{0:T(1024)} %param.12) | copy-start | bytes 12292
  47.0 5.4 %copy-start.8 = (f32[1024]{0:T(1024)S(1)}, f32[1024]{0:T(1024)}, u32[]{:S(2)}) copy-start(f32[1024]{0:T(1024)} %param.11) | copy-start | bytes 12292
  47.0 35.7 %all-to-all-start = ((bf16[64,16,1024]{2,1,0:T(8,128)(2,1)}), bf16[64,16,1024]{2,1,0:T(8,128)(2,1)S(1)}, u32[]{:S(2)}, u32[]{:S(2)}) async-start(bf16[64,16,1024]{2,1,0:T(8,128)(2,1)} %copy-done.2), calls=%async_computation | async-start | bytes 4194304 | tf_op jit(solution)/shard_map/all_to_all | solution.py:522
  52.4 30.3 %copy-start.3 = (s32[2,128]{1,0:T(2,128)}, s32[2,128]{1,0:T(2,128)S(1)}, u32[]{:S(2)}) copy-start(s32[2,128]{1,0:T(2,128)S(1)} %pad_add_fusion.order_ref) | copy-start | bytes 3076
  52.4 2.2 copy-start.5
  54.6 28.0 %copy-start.9 = (s32[1,256]{1,0:T(1,128)S(1)}, s32[1,256]{1,0:T(1,128)}, u32[]{:S(2)}) copy-start(s32[1,256]{1,0:T(1,128)} %slot_ref.1) | copy-start | bytes 3076
  78.5 1.3 copy-start.10
  79.8 1.4 copy-start.14
  81.2 1.3 copy-start.16
  82.7 1.6 copy-start.6
  84.2 1.6 copy-start.15
  101.0 6.7 %copy-start.11 = (bf16[4,256,1024]{2,1,0:T(8,128)(2,1)}, bf16[4,256,1024]{2,1,0:T(8,128)(2,1)S(1)}, u32[]{:S(2)}) copy-start(bf16[4,256,1024]{2,1,0:T(8,128)(2,1)S(1)} %get-tuple-element.35.grad_ref) | copy-start | bytes 6291460
  101.0 6.6 %copy-start.12 = (bf16[4,256,1024]{2,1,0:T(8,128)(2,1)}, bf16[4,256,1024]{2,1,0:T(8,128)(2,1)S(1)}, u32[]{:S(2)}) copy-start(bf16[4,256,1024]{2,1,0:T(8,128)(2,1)S(1)} %get-tuple-element.33.att_grad_ref) | copy-start | bytes 6291460
  101.0 6.6 %copy-start.13 = (bf16[4,256,1024]{2,1,0:T(8,128)(2,1)}, bf16[4,256,1024]{2,1,0:T(8,128)(2,1)S(1)}, u32[]{:S(2)}) copy-start(bf16[4,256,1024]{2,1,0:T(8,128)(2,1)S(1)} %get-tuple-element.34.val_grad_ref) | copy-start | bytes 6291460
  101.0 4.5 %collective-permute-start = (bf16[512,2048]{1,0:T(8,128)(2,1)S(1)}, bf16[512,2048]{1,0:T(8,128)(2,1)S(1)}, u32[]{:S(2)}, u32[]{:S(2)}) collective-permute-start(bf16[512,2048]{1,0:T(8,128)(2,1)S(1)} %get-tuple-element.30), channel_id=1, source_target_pairs={{0,2},{2,0},{1,3},{3,1},{4,6},{6,4},{5,7},{7,5},{8,10},{10,8},{9,1... | collective-permute-start | bytes 6291464 | tf_op jit(solution)/shard_map/ppermute | solution.py:509
  107.6 47.4 %all-to-all-start.2 = ((bf16[64,8,2048]{2,1,0:T(8,128)(2,1)}), bf16[64,8,2048]{2,1,0:T(8,128)(2,1)S(1)}, u32[]{:S(2)}, u32[]{:S(2)}) async-start(bf16[64,8,2048]{2,1,0:T(8,128)(2,1)} %bitcast.8), calls=%async_computation.2 | async-start | bytes 4194304 | tf_op jit(solution)/shard_map/all_to_all | solution.py:514
  155.1 1.3 copy-start.17
  156.4 4.6 %collective-permute-start.1 = (bf16[512,2176]{1,0:T(8,128)(2,1)}, bf16[512,2176]{1,0:T(8,128)(2,1)S(1)}, u32[]{:S(2)}, u32[]{:S(2)}) collective-permute-start(bf16[512,2176]{1,0:T(8,128)(2,1)} %get-tuple-element.42), channel_id=1, source_target_pairs={{0,2},{2,0},{1,3},{3,1},{4,6},{6,4},{5,7},{7,5},{8,10},{10,8},{9,1... | collective-permute-start | bytes 6684680 | tf_op jit(solution)/shard_map/ppermute | solution.py:503
  164.1 17.8 %collective-permute-start.2 = (bf16[256,2176]{1,0:T(8,128)(2,1)}, bf16[256,2176]{1,0:T(8,128)(2,1)}, u32[]{:S(2)}, u32[]{:S(2)}) collective-permute-start(bf16[256,2176]{1,0:T(8,128)(2,1)} %get-tuple-element.46), channel_id=1, source_target_pairs={{0,4},{2,14},{4,0},{6,10},{8,12},{10,6},{12,8},{14,2},{1,5},{3,15}... | collective-permute-start | bytes 3342344 | tf_op jit(solution)/shard_map/ppermute | solution.py:504
  165.7 45.0 %all-to-all-start.3 = ((bf16[64,16,1024]{2,1,0:T(8,128)(2,1)}), bf16[64,16,1024]{2,1,0:T(8,128)(2,1)S(1)}, u32[]{:S(2)}, u32[]{:S(2)}) async-start(bf16[64,16,1024]{2,1,0:T(8,128)(2,1)} %get-tuple-element.40), calls=%async_computation.3 | async-start | bytes 4194304 | tf_op jit(solution)/shard_map/all_to_all | solution.py:535
  183.1 25.5 %collective-permute-start.3 = (bf16[128,2176]{1,0:T(8,128)(2,1)S(1)}, bf16[128,2176]{1,0:T(8,128)(2,1)S(1)}, u32[]{:S(2)}, u32[]{:S(2)}) collective-permute-start(bf16[128,2176]{1,0:T(8,128)(2,1)S(1)} %add_convert_fusion.4), channel_id=1, source_target_pairs={{0,12},{2,6},{4,8},{6,2},{8,4},{10,14},{12,0},{14,10},{1,13},{3,7}... | collective-permute-start | bytes 1671176 | tf_op jit(solution)/shard_map/ppermute | solution.py:505
  210.7 18.5 %all-to-all-start.4 = ((bf16[16,8,2176]{2,1,0:T(8,128)(2,1)}), bf16[16,8,2176]{2,1,0:T(8,128)(2,1)S(1)}, u32[]{:S(2)}, u32[]{:S(2)}) async-start(bf16[16,8,2176]{2,1,0:T(8,128)(2,1)} %bitcast.3), calls=%async_computation.4 | async-start | bytes 1114112 | tf_op jit(solution)/shard_map/all_to_all | solution.py:514

commit v4 on v3

--- a/solution.py
+++ b/solution.py
@@ -332,7 +332,8 @@
 
 def scores_kernel(
     order_ref, joined_ref, weights_ref, natural_ref, proj_ref, att_grad_ref, val_grad_ref, grad_ref, places_ref, w_far, gain_ref,
-    turned_far, out_ref, keep_ref, send_ref, results, pairs, sums, terms, w_ref, turned_ref, arrived,
+    turned_far, out_far, keep_far, send_far,
+    results, pairs, sums, terms, w_ref, turned_ref, out_ref, keep_ref, send_ref, arrived, left,
 ):
     step = pl.program_id(0)
     copies = [
@@ -397,18 +398,34 @@
 
     @pl.when(step == pl.num_programs(0) - 1)
     def _():
+        leaving = []
+
+        def leave(near, far, where, value=None):
+            if value is not None:
+                near[where] = value
+            leaving.append(pltpu.make_async_copy(near.at[where], far.at[where], left.at[len(leaving)]))
+            leaving[-1].start()
+
         order = place_major_to(SQUARE)
         run = GROUP * SPAN
         for c in range(frames // run):
             chunk = results[:, c * run : (c + 1) * run, :].reshape(SQUARE[0], width)
             moved = mm(order, chunk).astype(BF)
-            out_ref[c * GROUP : (c + 1) * GROUP] = moved.reshape(GROUP, SPAN * SPAN, width)
+            leave(out_ref, out_far, slice(c * GROUP, (c + 1) * GROUP), moved.reshape(GROUP, SPAN * SPAN, width))
         chunk = terms.shape[1]
         for at in range(0, 2 * width, chunk):
-            terms[...] = mm(turned_ref[...], pairs[:, at : at + chunk])
-            place_rows(terms, order_ref, 1, keep_ref, send_ref, slice(at, at + chunk))
+            cols = slice(at, at + chunk)
+            terms[...] = mm(turned_ref[...], pairs[:, cols])
+            place_rows(terms, order_ref, 1, keep_ref, send_ref, cols)
+            leave(keep_ref, keep_far, (slice(None), cols))
+            leave(send_ref, send_far, (slice(None), cols))
+        cols = slice(2 * width, 2 * width + PAIR)
         terms[:, :PAIR] = jnp.concatenate([sums[...]] * (PAIR // sums.shape[0]), axis=0).T
-        place_rows(terms.at[:, :PAIR], order_ref, 1, keep_ref, send_ref, slice(2 * width, 2 * width + PAIR))
+        place_rows(terms.at[:, :PAIR], order_ref, 1, keep_ref, send_ref, cols)
+        leave(keep_ref, keep_far, (slice(None), cols))
+        leave(send_ref, send_far, (slice(None), cols))
+        for copy in leaving:
+            copy.wait()
 
 
 def scores_backward(order, joined, weights, natural, proj, att_grad, val_grad, grads, places, w_qkv, gain, turned):
@@ -428,7 +445,7 @@
                       per(frames, 3 * width),
                       per(frames, width), per(frames, width), per(frames, width), per(frames, width),
                       pl.BlockSpec(memory_space=pl.ANY), full((1, width)), pl.BlockSpec(memory_space=pl.ANY)],
-            out_specs=[full(o.shape) for o in outs],
+            out_specs=[pl.BlockSpec(memory_space=pl.ANY)] * len(outs),
             scratch_shapes=[
                 pltpu.VMEM((SPAN, frames, width), BF),
                 pltpu.VMEM((tokens, 2 * width), BF),
@@ -436,7 +453,9 @@
                 pltpu.VMEM((width, 256), F32),
                 pltpu.VMEM(w_qkv.shape, BF),
                 pltpu.VMEM(turned.shape, BF),
+                *[pltpu.VMEM(o.shape, BF) for o in outs],
                 pltpu.SemaphoreType.DMA((2,)),
+                pltpu.SemaphoreType.DMA((32,)),
             ],
         ),
         out_shape=outs,

time: 232 us -> 231 us (level)
  no operation moved by 1% of the time
where the time goes in v4:
time: 231 us; the launch traced here: 230 us
  Pallas kernels  82.2 us (36%)
  waiting for transfers between devices  68.1 us (29%)
  starting transfers between devices  50.1 us (22%)
  local copies, waits for them, and re-layouts  17.3 us (7%)
  other arithmetic  11.2 us (5%)
    pallas_call x1, Pallas kernels, scores_backward(): pl.pallas_call(scores_kernel, grid_spec=pltpu.PrefetchScalarGridSpec(num_...  36.3 us
    all_to_all x1, waiting for transfers between devices, on_device(): rows_in = lax.all_to_all(split_patches(layer_input), SEQ, 0, 0, tiled=True)  24.9 us
    pallas_call x1, Pallas kernels, forward(): pl.pallas_call(forward_kernel, grid=(SPAN,), in_specs=[full(rows.shape),...  23.9 us
    ppermute x1, waiting for transfers between devices, sum_along_x(): return add(keep, lax.ppermute(send, ('x', 'core'), neighbours(1)))  20.6 us
    all_to_all x2, starting transfers between devices, to_owners(): lax.all_to_all(joined.reshape(count, rows // count, columns), axes, 0, 0,...  17.2 us
    unnamed x40, local copies, waits for them, and re-layouts  16 us
    pallas_call x1, Pallas kernels, values_backward(): pl.pallas_call(values_kernel, grid_spec=pltpu.PrefetchScalarGridSpec(num_...  15.1 us
    all_to_all x1, starting transfers between devices, on_device(): rows_in = lax.all_to_all(split_patches(layer_input), SEQ, 0, 0, tiled=True)  11.7 us
  transfers between devices with their start and end apart: 9, of which 7 were waited for; matrix products, arithmetic and copies ran while one was open for 3% of the time, Pallas kernels for 28%

profile of v4, /device:TPU:0, one launch (start us, length us, event | category | flops | bytes accessed | tf_op | source)
XLA Modules:
  0.0 229.7 jit_solution(9773566364179502373)
XLA Ops:
  0.6 1.6 copy-done
  2.2 2.7 %split_patches.1 = bf16[64,16,1024]{2,1,0:T(8,128)(2,1)} custom-call(bf16[1,4,256,1024]{3,2,1,0:T(8,128)(2,1)S(1)} %copy-done), custom_call_target="tpu_custom_call" | custom-call | flops 536870912 | bytes 4194304 | tf_op jit(solution)/shard_map/split_patches/pallas_call | solution.py:89
  4.9 11.7 %all-to-all-start.1 = ((bf16[64,16,1024]{2,1,0:T(8,128)(2,1)}), bf16[64,16,1024]{2,1,0:T(8,128)(2,1)}, u32[]{:S(2)}, u32[]{:S(2)}) async-start(bf16[64,16,1024]{2,1,0:T(8,128)(2,1)} %split_patches.1), calls=%async_computation.1 | async-start | bytes 4194304 | tf_op jit(solution)/shard_map/all_to_all | solution.py:539
  16.7 0.3 reverse
  17.0 0.1 slice.76
  17.1 1.7 prepare.1
  18.8 0.0 copy-start.2
  18.8 1.3 copy-done.2
  20.1 2.0 copy-done.4
  22.0 24.9 %all-to-all-done.1.rows_ref = bf16[64,16,1024]{2,1,0:T(8,128)(2,1)} async-done(((bf16[64,16,1024]{2,1,0:T(8,128)(2,1)}), bf16[64,16,1024]{2,1,0:T(8,128)(2,1)}, u32[]{:S(2)}, u32[]{:S(2)}) %all-to-all-start.1) | async-done | bytes 2097184 | tf_op jit(solution)/shard_map/all_to_all | solution.py:539
  47.0 5.4 %all-to-all-start = ((bf16[64,16,1024]{2,1,0:T(8,128)(2,1)}), bf16[64,16,1024]{2,1,0:T(8,128)(2,1)S(1)}, u32[]{:S(2)}, u32[]{:S(2)}) async-start(bf16[64,16,1024]{2,1,0:T(8,128)(2,1)} %copy-done.2), calls=%async_computation | async-start | bytes 4194304 | tf_op jit(solution)/shard_map/all_to_all | solution.py:541
  52.4 0.0 copy-start.3
  52.4 2.2 copy-done.5
  54.6 23.9 %forward.1 = (bf16[4,256,1024]{2,1,0:T(8,128)(2,1)S(1)}, bf16[1024,1024]{1,0:T(8,128)(2,1)S(1)}, bf16[4,256,3072]{2,1,0:T(8,128)(2,1)}, bf16[4,16,256,256]{3,2,1...) custom-call(bf16[64,16,1024]{2,1,0:T(8,128)(2,1)} %all-to-all-done.1.rows_ref, ...), custom_call_target="tpu_custom_call" | custom-call | flops 16000000000 | bytes 35651584 | tf_op jit(solution)/shard_map/forward/pallas_call | solution.py:224
  78.5 1.3 copy-done.10
  79.8 1.4 copy-done.14
  81.2 1.3 copy-done.16
  82.5 0.1 all-to-all-done.rows_ref
  82.7 1.6 copy-done.6
  84.3 1.6 copy-done.15
  85.8 15.1 %values_backward.1 = (bf16[4,256,1024]{2,1,0:T(8,128)(2,1)S(1)}, bf16[4,256,1024]{2,1,0:T(8,128)(2,1)S(1)}, bf16[4,256,1024]{2,1,0:T(8,128)(2,1)S(1)}, bf16[512,...) custom-call(s32[2,128]{1,0:T(2,128)S(1)} %pad_add_fusion.order_ref, bf16[64,16,1024]{2,1,0:T(8,128)(2,1)S(1)} %all-to-all-done.rows_ref, ...), custom_call_target="tpu_custom_call" | custom-call | flops 12000000000 | bytes 29360128 | tf_op jit(solution)/shard_map/values_backward/pallas_call | solution.py:311
  101.0 0.7 collective-permute-start
  101.7 3.8 %collective-permute-done = bf16[512,2048]{1,0:T(8,128)(2,1)S(1)} collective-permute-done((bf16[512,2048]{1,0:T(8,128)(2,1)S(1)}, bf16[512,2048]{1,0:T(8,128)(2,1)S(1)}, u32[]{:S(2)}, u32[]{:S(2)}) %collective-permute-start) | collective-permute-done | bytes 2097184 | tf_op jit(solution)/shard_map/ppermute | solution.py:528
  105.5 2.1 add_convert_fusion.joined_ref
  107.6 10.2 %all-to-all-start.2 = ((bf16[64,8,2048]{2,1,0:T(8,128)(2,1)}), bf16[64,8,2048]{2,1,0:T(8,128)(2,1)S(1)}, u32[]{:S(2)}, u32[]{:S(2)}) async-start(bf16[64,8,2048]{2,1,0:T(8,128)(2,1)} %bitcast.8), calls=%async_computation.2 | async-start | bytes 4194304 | tf_op jit(solution)/shard_map/all_to_all | solution.py:533
  117.8 36.3 %scores_backward.1 = (bf16[64,16,1024]{2,1,0:T(8,128)(2,1)}, bf16[512,2176]{1,0:T(8,128)(2,1)}, bf16[512,2176]{1,0:T(8,128)(2,1)}) custom-call(s32[2,128]{1,0:T(2,128)} %copy-done.3, bf16[512,2048]{1,0:T(8,128)(2,1)} %add_convert_fusion.joined_ref, bf16[4,16,256,256]{3,2,1,0:T(8,128)(2,1)} %get-tuple-element.26.weights_ref, ...), custom_call_target="tpu_custom_call" | custom-call | flops 24000000000 | bytes 35651584 | tf_op jit(solution)/shard_map/scores_backward/pallas_call | solution.py:439
  154.1 0.0 all-to-all-done.2.refs_0_
  154.1 0.0 copy-start.17
  154.2 1.3 copy-done.17
  155.5 0.0 collective-permute-start.1
  155.5 4.6 %collective-permute-done.1 = bf16[512,2176]{1,0:T(8,128)(2,1)S(1)} collective-permute-done((bf16[512,2176]{1,0:T(8,128)(2,1)}, bf16[512,2176]{1,0:T(8,128)(2,1)S(1)}, u32[]{:S(2)}, u32[]{:S(2)}) %collective-permute-start.1) | collective-permute-done | bytes 2228256 | tf_op jit(solution)/shard_map/ppermute | solution.py:522
  160.0 3.2 %add_convert_fusion.2 = (bf16[256,2176]{1,0:T(8,128)(2,1)S(1)}, bf16[256,2176]{1,0:T(8,128)(2,1)}) fusion(bf16[512,2176]{1,0:T(8,128)(2,1)S(1)} %collective-permute-done.1, bf16[512,2176]{1,0:T(8,128)(2,1)} %get-tuple-element.41), kind=kLoop, calls=%fused_computation.3 | loop fusion | flops 4456448 | bytes 6684672 | tf_op jit(solution)/shard_map/convert_element_type | solution.py:513
  163.2 1.6 collective-permute-start.2
  164.8 10.2 %all-to-all-start.3 = ((bf16[64,16,1024]{2,1,0:T(8,128)(2,1)}), bf16[64,16,1024]{2,1,0:T(8,128)(2,1)S(1)}, u32[]{:S(2)}, u32[]{:S(2)}) async-start(bf16[64,16,1024]{2,1,0:T(8,128)(2,1)} %get-tuple-element.40), calls=%async_computation.3 | async-start | bytes 4194304 | tf_op jit(solution)/shard_map/all_to_all | solution.py:554
  175.0 5.7 %collective-permute-done.2 = bf16[256,2176]{1,0:T(8,128)(2,1)} collective-permute-done((bf16[256,2176]{1,0:T(8,128)(2,1)}, bf16[256,2176]{1,0:T(8,128)(2,1)}, u32[]{:S(2)}, u32[]{:S(2)}) %collective-permute-start.2) | collective-permute-done | bytes 1114144 | tf_op jit(solution)/shard_map/ppermute | solution.py:523
  180.7 1.2 add_convert_fusion.4
  181.9 3.3 %collective-permute-start.3 = (bf16[128,2176]{1,0:T(8,128)(2,1)S(1)}, bf16[128,2176]{1,0:T(8,128)(2,1)S(1)}, u32[]{:S(2)}, u32[]{:S(2)}) collective-permute-start(bf16[128,2176]{1,0:T(8,128)(2,1)S(1)} %add_convert_fusion.4), channel_id=1, source_target_pairs={{0,12},{2,6},{4,8},{6,2},{8,4},{10,14},{12,0},{14,10},{1,13},{3,7}... | collective-permute-start | bytes 1671176 | tf_op jit(solution)/shard_map/ppermute | solution.py:524
  185.2 1.9 convert_reduce_fusion
  187.1 20.6 %collective-permute-done.3 = bf16[128,2176]{1,0:T(8,128)(2,1)S(1)} collective-permute-done((bf16[128,2176]{1,0:T(8,128)(2,1)S(1)}, bf16[128,2176]{1,0:T(8,128)(2,1)S(1)}, u32[]{:S(2)}, u32[]{:S(2)}) %collective-permute-start.3) | collective-permute-done | bytes 557088 | tf_op jit(solution)/shard_map/ppermute | solution.py:524
  207.7 2.1 add_convert_fusion.3.refs_1_
  209.8 0.0 all-to-all-done.3.rows_ref.refs_0_
  209.8 7.0 %all-to-all-start.4 = ((bf16[16,8,2176]{2,1,0:T(8,128)(2,1)}), bf16[16,8,2176]{2,1,0:T(8,128)(2,1)S(1)}, u32[]{:S(2)}, u32[]{:S(2)}) async-start(bf16[16,8,2176]{2,1,0:T(8,128)(2,1)} %bitcast.3), calls=%async_computation.4 | async-start | bytes 1114112 | tf_op jit(solution)/shard_map/all_to_all | solution.py:533
  216.8 0.6 fusion.8
  217.5 2.5 %merge_patches.1 = bf16[1,4,256,1024]{3,2,1,0:T(8,128)(2,1)} custom-call(bf16[64,16,1024]{2,1,0:T(8,128)(2,1)S(1)} %all-to-all-done.3.rows_ref.refs_0_), custom_call_target="tpu_custom_call" | custom-call | flops 536870912 | bytes 4194304 | tf_op jit(solution)/shard_map/merge_patches/pallas_call | solution.py:108
  220.0 8.3 %all-to-all-done.4 = bf16[16,8,2176]{2,1,0:T(8,128)(2,1)S(1)} async-done(((bf16[16,8,2176]{2,1,0:T(8,128)(2,1)}), bf16[16,8,2176]{2,1,0:T(8,128)(2,1)S(1)}, u32[]{:S(2)}, u32[]{:S(2)}) %all-to-all-start.4) | async-done | bytes 557088 | tf_op jit(solution)/shard_map/all_to_all | solution.py:533
  228.3 0.1 convert_reduce_fusion.1
  228.4 0.7 slice_reduce_fusion
  229.1 0.6 pad_maximum_fusion
  (34 shorter events, 0.1 us)
Async XLA Ops:
  0.6 1.6 copy-start
  4.9 11.7 %copy-start.18 = (f32[16,511]{1,0:T(8,128)S(1)}, f32[16,511]{1,0:T(8,128)}, u32[]{:S(2)}) copy-start(f32[16,511]{1,0:T(8,128)} %param.15) | copy-start | bytes 98116
  4.9 12.2 %copy-start.1 = (bf16[1,4,256,1024]{3,2,1,0:T(8,128)(2,1)S(1)}, bf16[1,4,256,1024]{3,2,1,0:T(8,128)(2,1)}, u32[]{:S(2)}) copy-start(bf16[1,4,256,1024]{3,2,1,0:T(8,128)(2,1)} %rows_ref.2) | copy-start | bytes 6291460
  4.9 42.1 %all-to-all-start.1 = ((bf16[64,16,1024]{2,1,0:T(8,128)(2,1)}), bf16[64,16,1024]{2,1,0:T(8,128)(2,1)}, u32[]{:S(2)}, u32[]{:S(2)}) async-start(bf16[64,16,1024]{2,1,0:T(8,128)(2,1)} %split_patches.1), calls=%async_computation.1 | async-start | bytes 4194304 | tf_op jit(solution)/shard_map/all_to_all | solution.py:539
  18.8 1.3 copy-start.2
  20.1 2.0 copy-start.4
  47.0 5.4 %copy-start.7 = (f32[1024]{0:T(1024)S(1)}, f32[1024]{0:T(1024)}, u32[]{:S(2)}) copy-start(f32[1024]{0:T(1024)} %param.12) | copy-start | bytes 12292
  47.0 5.4 %copy-start.8 = (f32[1024]{0:T(1024)S(1)}, f32[1024]{0:T(1024)}, u32[]{:S(2)}) copy-start(f32[1024]{0:T(1024)} %param.11) | copy-start | bytes 12292
  47.0 35.7 %all-to-all-start = ((bf16[64,16,1024]{2,1,0:T(8,128)(2,1)}), bf16[64,16,1024]{2,1,0:T(8,128)(2,1)S(1)}, u32[]{:S(2)}, u32[]{:S(2)}) async-start(bf16[64,16,1024]{2,1,0:T(8,128)(2,1)} %copy-done.2), calls=%async_computation | async-start | bytes 4194304 | tf_op jit(solution)/shard_map/all_to_all | solution.py:541
  52.4 30.3 %copy-start.3 = (s32[2,128]{1,0:T(2,128)}, s32[2,128]{1,0:T(2,128)S(1)}, u32[]{:S(2)}) copy-start(s32[2,128]{1,0:T(2,128)S(1)} %pad_add_fusion.order_ref) | copy-start | bytes 3076
  52.4 2.2 copy-start.5
  54.6 28.0 %copy-start.9 = (s32[1,256]{1,0:T(1,128)S(1)}, s32[1,256]{1,0:T(1,128)}, u32[]{:S(2)}) copy-start(s32[1,256]{1,0:T(1,128)} %slot_ref.1) | copy-start | bytes 3076
  78.5 1.3 copy-start.10
  79.8 1.4 copy-start.14
  81.2 1.3 copy-start.16
  82.7 1.6 copy-start.6
  84.2 1.6 copy-start.15
  101.0 6.7 %copy-start.11 = (bf16[4,256,1024]{2,1,0:T(8,128)(2,1)}, bf16[4,256,1024]{2,1,0:T(8,128)(2,1)S(1)}, u32[]{:S(2)}) copy-start(bf16[4,256,1024]{2,1,0:T(8,128)(2,1)S(1)} %get-tuple-element.35.grad_ref) | copy-start | bytes 6291460
  101.0 6.6 %copy-start.12 = (bf16[4,256,1024]{2,1,0:T(8,128)(2,1)}, bf16[4,256,1024]{2,1,0:T(8,128)(2,1)S(1)}, u32[]{:S(2)}) copy-start(bf16[4,256,1024]{2,1,0:T(8,128)(2,1)S(1)} %get-tuple-element.33.att_grad_ref) | copy-start | bytes 6291460
  101.0 6.6 %copy-start.13 = (bf16[4,256,1024]{2,1,0:T(8,128)(2,1)}, bf16[4,256,1024]{2,1,0:T(8,128)(2,1)S(1)}, u32[]{:S(2)}) copy-start(bf16[4,256,1024]{2,1,0:T(8,128)(2,1)S(1)} %get-tuple-element.34.val_grad_ref) | copy-start | bytes 6291460
  101.0 4.5 %collective-permute-start = (bf16[512,2048]{1,0:T(8,128)(2,1)S(1)}, bf16[512,2048]{1,0:T(8,128)(2,1)S(1)}, u32[]{:S(2)}, u32[]{:S(2)}) collective-permute-start(bf16[512,2048]{1,0:T(8,128)(2,1)S(1)} %get-tuple-element.30), channel_id=1, source_target_pairs={{0,2},{2,0},{1,3},{3,1},{4,6},{6,4},{5,7},{7,5},{8,10},{10,8},{9,1... | collective-permute-start | bytes 6291464 | tf_op jit(solution)/shard_map/ppermute | solution.py:528
  107.6 46.5 %all-to-all-start.2 = ((bf16[64,8,2048]{2,1,0:T(8,128)(2,1)}), bf16[64,8,2048]{2,1,0:T(8,128)(2,1)S(1)}, u32[]{:S(2)}, u32[]{:S(2)}) async-start(bf16[64,8,2048]{2,1,0:T(8,128)(2,1)} %bitcast.8), calls=%async_computation.2 | async-start | bytes 4194304 | tf_op jit(solution)/shard_map/all_to_all | solution.py:533
  154.1 1.3 copy-start.17
  155.5 4.6 %collective-permute-start.1 = (bf16[512,2176]{1,0:T(8,128)(2,1)}, bf16[512,2176]{1,0:T(8,128)(2,1)S(1)}, u32[]{:S(2)}, u32[]{:S(2)}) collective-permute-start(bf16[512,2176]{1,0:T(8,128)(2,1)} %get-tuple-element.42), channel_id=1, source_target_pairs={{0,2},{2,0},{1,3},{3,1},{4,6},{6,4},{5,7},{7,5},{8,10},{10,8},{9,1... | collective-permute-start | bytes 6684680 | tf_op jit(solution)/shard_map/ppermute | solution.py:522
  163.2 17.5 %collective-permute-start.2 = (bf16[256,2176]{1,0:T(8,128)(2,1)}, bf16[256,2176]{1,0:T(8,128)(2,1)}, u32[]{:S(2)}, u32[]{:S(2)}) collective-permute-start(bf16[256,2176]{1,0:T(8,128)(2,1)} %get-tuple-element.46), channel_id=1, source_target_pairs={{0,4},{2,14},{4,0},{6,10},{8,12},{10,6},{12,8},{14,2},{1,5},{3,15}... | collective-permute-start | bytes 3342344 | tf_op jit(solution)/shard_map/ppermute | solution.py:523
  164.8 45.0 %all-to-all-start.3 = ((bf16[64,16,1024]{2,1,0:T(8,128)(2,1)}), bf16[64,16,1024]{2,1,0:T(8,128)(2,1)S(1)}, u32[]{:S(2)}, u32[]{:S(2)}) async-start(bf16[64,16,1024]{2,1,0:T(8,128)(2,1)} %get-tuple-element.40), calls=%async_computation.3 | async-start | bytes 4194304 | tf_op jit(solution)/shard_map/all_to_all | solution.py:554
  181.9 25.8 %collective-permute-start.3 = (bf16[128,2176]{1,0:T(8,128)(2,1)S(1)}, bf16[128,2176]{1,0:T(8,128)(2,1)S(1)}, u32[]{:S(2)}, u32[]{:S(2)}) collective-permute-start(bf16[128,2176]{1,0:T(8,128)(2,1)S(1)} %add_convert_fusion.4), channel_id=1, source_target_pairs={{0,12},{2,6},{4,8},{6,2},{8,4},{10,14},{12,0},{14,10},{1,13},{3,7}... | collective-permute-start | bytes 1671176 | tf_op jit(solution)/shard_map/ppermute | solution.py:524
  209.8 18.5 %all-to-all-start.4 = ((bf16[16,8,2176]{2,1,0:T(8,128)(2,1)}), bf16[16,8,2176]{2,1,0:T(8,128)(2,1)S(1)}, u32[]{:S(2)}, u32[]{:S(2)}) async-start(bf16[16,8,2176]{2,1,0:T(8,128)(2,1)} %bitcast.3), calls=%async_computation.4 | async-start | bytes 1114112 | tf_op jit(solution)/shard_map/all_to_all | solution.py:533
